TPU v7x, 32 devices: a whole 2x2x4 slice. The times are simulated.
32 devices in a mesh: node: 8 (over y, x, core), local: 4 (over z).
Axes of the slice: x: 2, y: 2, z: 4, core: 2. Of those that a mesh axis runs over, the one named last changes fastest.
Arguments:
- grads: bfloat16 [4096, 5376], P(('node', 'local')), may hold values from -6 to 6
- token_slot: int32 [4096], P(('node', 'local')), may hold values from 0 to 63, as said below
- node_ids: int32 [8, 64], P('node', 'local'), may hold values from 0 to 262143, as said below
- touched_ids: int32 [512], P(('node', 'local')), may hold values from -1 to 262143, as said below
- owner_map: int32 [32, 8, 2], P(('node', 'local')), may hold values from -1 to 15, as said below
- moment: float32 [512, 5376], P(('node', 'local')), may hold values from -4 to 4
- second: float32 [512, 5376], P(('node', 'local')), may hold values from 0.01 to 1
- master: float32 [512, 5376], P(('node', 'local')), may hold values from -0.12 to 0.12
Outputs:
- token_rows: bfloat16 [4096, 5376], P(('node', 'local'))
- moment_out: float32 [512, 5376], P(('node', 'local'))
- second_out: float32 [512, 5376], P(('node', 'local'))
- master_out: float32 [512, 5376], P(('node', 'local'))
Inputs may be any that keep to these rules, and one draw needn't show every extreme that they name: `node_ids`: within one device's 16 entries the ids are distinct and at most 2 of them share an owner node id // 32768; for each local index one owner node receives exactly 2 ids from every node's device of that local index. `token_slot`: every entry of a node's list is used by some token of that node. `touched_ids`: on device (o, j) the entries that are not -1 are distinct ids with owner node o, and they are exactly the ids that devices of local index j list with owner node o. `owner_map`: on device (o, j), entry [n, c] is the position in this device's touched_ids of the c-th id, in list order, that device (n, j) lists with owner node o, and -1 where device (n, j) lists fewer than c + 1 such ids.
All inputs are finite; a program needn't handle non-finite values.
Results may differ from a plain program's by a relative error of at most 0.014.
Values may be sent and summed in bfloat16 or wider, within the bound.
A program may use at most 64 MiB of HBM per device.

v0:
```python
import jax
import jax.numpy as jnp
from jax import lax
from jax.sharding import PartitionSpec as P

VOCAB = 262144
STEP = 100


BETA_ONE = 0.9
BETA_TWO = 0.999
LEARN_RATE = 0.01
EPSILON = 1e-08


def adam_rows(gradient, moment, second, master, alive_rows):
    corr_one = 1.0 - BETA_ONE**STEP
    corr_two = 1.0 - BETA_TWO**STEP
    moment_new = BETA_ONE * moment + (1.0 - BETA_ONE) * gradient
    second_new = BETA_TWO * second + (1.0 - BETA_TWO) * gradient * gradient
    master_new = master - LEARN_RATE * (moment_new / corr_one) / (
        jnp.sqrt(second_new / corr_two) + EPSILON
    )
    kept = alive_rows[:, None]
    return (
        jnp.where(kept, moment_new, moment),
        jnp.where(kept, second_new, second),
        jnp.where(kept, master_new, master),
    )


def on_device(grads, token_slot, node_ids, touched_ids, owner_map, moment, second, master):
    slot_dev = node_ids.shape[1]
    width = grads.shape[1]
    node_count = lax.axis_size("node")
    capacity = owner_map.shape[2]
    touch_cap = touched_ids.shape[0]
    wanted = lax.iota(jnp.int32, slot_dev * lax.axis_size("local"))
    selector = (wanted[:, None] == token_slot[None, :]).astype(jnp.bfloat16)
    node_sum = lax.psum_scatter(
        jnp.dot(selector, grads, preferred_element_type=jnp.float32).astype(jnp.bfloat16),
        "local",
        scatter_dimension=0,
        tiled=True,
    )
    owner_node = node_ids[0] // (VOCAB // node_count)
    same_owner = owner_node[:, None] == owner_node[None, :]
    positions = lax.iota(jnp.int32, slot_dev)
    earlier = positions[None, :] < positions[:, None]
    rank_slot = jnp.sum((same_owner & earlier).astype(jnp.int32), axis=1)
    send_slot = owner_node * capacity + rank_slot
    route_map = (lax.iota(jnp.int32, node_count * capacity)[:, None] == send_slot[None, :]).astype(
        jnp.bfloat16
    )
    outgoing = jnp.dot(route_map, node_sum, preferred_element_type=jnp.float32).astype(jnp.bfloat16)
    incoming = lax.all_to_all(
        outgoing.reshape(node_count, capacity, width),
        "node",
        split_axis=0,
        concat_axis=0,
        tiled=True,
    )
    position_map = owner_map.reshape(-1)
    collect = (lax.iota(jnp.int32, touch_cap)[:, None] == position_map[None, :]).astype(
        jnp.bfloat16
    )
    gradient = jnp.dot(
        collect, incoming.reshape(node_count * capacity, width), preferred_element_type=jnp.float32
    )
    moment_out, second_out, master_out = adam_rows(
        gradient, moment, second, master, touched_ids >= 0
    )
    fresh_rows = master_out.astype(jnp.bfloat16)
    reply_rows = lax.dot_general(
        collect, fresh_rows, (((0,), (0,)), ((), ())), preferred_element_type=jnp.float32
    ).astype(jnp.bfloat16)
    returned = lax.all_to_all(
        reply_rows.reshape(node_count, capacity, width),
        "node",
        split_axis=0,
        concat_axis=0,
        tiled=True,
    )
    listed_rows = lax.dot_general(
        route_map,
        returned.reshape(node_count * capacity, width),
        (((0,), (0,)), ((), ())),
        preferred_element_type=jnp.float32,
    ).astype(jnp.bfloat16)
    shard_rows = lax.all_gather(listed_rows, "local", axis=0, tiled=True)
    wanted = lax.iota(jnp.int32, shard_rows.shape[0])
    selector = (token_slot[:, None] == wanted[None, :]).astype(jnp.bfloat16)
    token_rows = jnp.dot(selector, shard_rows, preferred_element_type=jnp.float32)
    return (token_rows.astype(jnp.bfloat16), moment_out, second_out, master_out)


def solution(mesh):
    placed = (
        P(("node", "local"), None),
        P(("node", "local")),
        P("node", "local"),
        P(("node", "local")),
        P(("node", "local"), None, None),
        P(("node", "local"), None),
        P(("node", "local"), None),
        P(("node", "local"), None),
    )
    return jax.shard_map(
        on_device,
        mesh=mesh,
        in_specs=placed,
        out_specs=(
            P(("node", "local"), None),
            P(("node", "local"), None),
            P(("node", "local"), None),
            P(("node", "local"), None),
        ),
        check_vma=False,
    )
```

profile of v0, /device:TPU:0, one launch (start us, length us, event | category | flops | bytes accessed | tf_op | source)
XLA Modules:
  0.0 83.5 jit_solution(12246174628953032083)
XLA Ops:
  7.2 0.0 copy-start
  7.2 0.0 copy-start.3
  7.2 0.0 copy-start.7
  7.2 0.0 reduce-scatter.2.cloned.1.call-start
  7.2 1.3 %copy-done = bf16[128,5376]{1,0:T(8,128)(2,1)S(1)} copy-done((bf16[128,5376]{1,0:T(8,128)(2,1)S(1)}, bf16[128,5376]{1,0:T(8,128)(2,1)}, u32[]{:S(2)}) %copy-start) | copy-done | bytes 1376280
  8.5 1.8 %convolution_convert_fusion.1 = bf16[64,5376]{1,0:T(8,128)(2,1)} fusion(bf16[128,5376]{1,0:T(8,128)(2,1)S(1)} %copy-done, s32[128]{0:T(128)} %param.9), kind=kOutput, calls=%fused_computation.1 | convolution fusion | flops 88432640 | bytes 2064896 | tf_op jit(solution)/shard_map/dot_general | solution.py:41
  10.4 0.0 reduce-scatter.2.cloned.1.call-update
  10.4 0.0 copy-done.3
  10.4 0.1 copy.14
  10.5 0.1 eq.86
  10.6 0.0 copy-done.7
  10.6 0.2 convert_reduce_fusion
  10.8 25.4 %reduce-scatter.2.cloned.1.call-done = bf16[16,5376]{1,0:T(8,128)(2,1)} async-done(((bf16[64,5376]{1,0:T(8,128)(2,1)}), bf16[16,5376]{1,0:T(8,128)(2,1)}) %reduce-scatter.2.cloned.1.call-update) | async-done | bytes 172048 | tf_op jit(solution)/shard_map/reduce_scatter | solution.py:40
  36.2 1.1 %convolution_convert_fusion.4 = bf16[16,5376]{1,0:T(8,128)(2,1)S(1)} fusion(bf16[16,5376]{1,0:T(8,128)(2,1)} %reduce-scatter.2.cloned.1.call-done, s32[16]{0:T(128)S(1)} %fusion.12), kind=kOutput, calls=%fused_computation.4 | convolution fusion | flops 2838784 | bytes 344128 | tf_op jit(solution)/shard_map/dot_general | solution.py:55
  37.3 0.7 reshape.53
  38.0 3.6 %all-to-all-start = ((bf16[8,2,5376]{2,1,0:T(2,128)(2,1)}), bf16[8,2,5376]{2,1,0:T(2,128)(2,1)S(1)}, u32[]{:S(2)}, u32[]{:S(2)}) async-start(bf16[8,2,5376]{2,1,0:T(2,128)(2,1)} %reshape.53), calls=%async_computation.1 | async-start | bytes 344064 | tf_op jit(solution)/shard_map/all_to_all | solution.py:56
  41.6 0.0 copy-done.8
  41.6 6.0 %all-to-all-done = bf16[8,2,5376]{2,1,0:T(2,128)(2,1)S(1)} async-done(((bf16[8,2,5376]{2,1,0:T(2,128)(2,1)}), bf16[8,2,5376]{2,1,0:T(2,128)(2,1)S(1)}, u32[]{:S(2)}, u32[]{:S(2)}) %all-to-all-start) | async-done | bytes 172064 | tf_op jit(solution)/shard_map/all_to_all | solution.py:56
  47.6 0.1 reshape.54
  47.7 0.0 copy-done.4
  47.7 0.0 copy-done.5
  47.7 0.0 copy-done.6
  47.7 1.2 %fusion.2 = (f32[16,5376]{1,0:T(8,128)}, f32[16,5376]{1,0:T(8,128)S(1)}, f32[16,5376]{1,0:T(8,128)}) fusion(f32[16,5376]{1,0:T(8,128)S(1)} %copy-done.4, pred[16]{0:T(512)(128)(4,1)S(1)} %broadcast_compare_fusion, f32[16,5376]{1,0:T(8,128)S(1)} %copy-done.5, f32[16,5376]{1,0:T(8,128)S(1)} %copy-done.6, bf16[16,5376]{1,0:T(8,128)(2,1)S(1)} %reshape.54, ...), kind=kOutput, calls=%fused_computation.10 | convolution fusion | flops 4043008 | bytes 2236496 | tf_op jit(solution)/shard_map/dot_general | solution.py:67
  48.9 0.2 convolution_convert_fusion.3
  49.2 0.1 reshape.55
  49.3 8.4 %all_to_all.10 = bf16[8,2,5376]{2,1,0:T(2,128)(2,1)S(1)} all-to-all(bf16[8,2,5376]{2,1,0:T(2,128)(2,1)S(1)} %reshape.55), channel_id=1, replica_groups=mesh['node'=8,'local'=4] {'node'}, dimensions={0} | all-to-all | bytes 344064 | tf_op jit(solution)/shard_map/all_to_all | solution.py:77
  57.6 0.1 reshape.56
  57.7 0.2 convolution_convert_fusion.2
  57.9 17.1 %all_gather.3 = bf16[64,5376]{1,0:T(8,128)(2,1)S(1)} all-gather(bf16[16,5376]{1,0:T(8,128)(2,1)S(1)} %convolution_convert_fusion.2), channel_id=1, replica_groups=mesh['node'=8,'local'=4] {'local'}, dimensions={0}, use_global_device_ids=true | all-gather | bytes 860160 | tf_op jit(solution)/shard_map/all_gather | solution.py:90
  75.0 0.0 copy-done.1
  75.0 0.0 copy-done.2
  75.0 1.6 %convolution_convert_fusion = bf16[128,5376]{1,0:T(8,128)(2,1)} fusion(bf16[64,5376]{1,0:T(8,128)(2,1)S(1)} %all_gather.3, s32[128]{0:T(128)S(1)} %copy-done.2), kind=kOutput, calls=%fused_computation | convolution fusion | flops 88776704 | bytes 2064896 | tf_op jit(solution)/shard_map/dot_general | solution.py:93
  (10 shorter events, 0.0 us)
Async XLA Ops:
  7.2 1.3 %copy-start = (bf16[128,5376]{1,0:T(8,128)(2,1)S(1)}, bf16[128,5376]{1,0:T(8,128)(2,1)}, u32[]{:S(2)}) copy-start(bf16[128,5376]{1,0:T(8,128)(2,1)} %param.8) | copy-start | bytes 4128772
  7.2 3.2 %copy-start.3 = (s32[1,8,2]{1,2,0:T(2,128)S(1)}, s32[1,8,2]{1,2,0:T(2,128)}, u32[]{:S(2)}) copy-start(s32[1,8,2]{1,2,0:T(2,128)} %param.12) | copy-start | bytes 196
  7.2 3.4 %copy-start.7 = (s32[1,16]{1,0:T(1,128)S(1)}, s32[1,16]{1,0:T(1,128)}, u32[]{:S(2)}) copy-start(s32[1,16]{1,0:T(1,128)} %param.10) | copy-start | bytes 196
  7.2 29.0 %reduce-scatter.2.cloned.1.call-start = ((), (), s32[]{:S(2)}) async-start(), calls=%async_computation.3 | async-start | bytes 860160 | tf_op jit(solution)/shard_map/reduce_scatter | solution.py:40
  10.4 31.3 %copy-start.8 = (s32[16]{0:T(128)S(1)}, s32[16]{0:T(128)}, u32[]{:S(2)}) copy-start(s32[16]{0:T(128)} %param.11) | copy-start | bytes 196
  10.4 37.3 %copy-start.4 = (f32[16,5376]{1,0:T(8,128)S(1)}, f32[16,5376]{1,0:T(8,128)}, u32[]{:S(2)}) copy-start(f32[16,5376]{1,0:T(8,128)} %param.14) | copy-start | bytes 1032196
  10.4 37.3 %copy-start.5 = (f32[16,5376]{1,0:T(8,128)S(1)}, f32[16,5376]{1,0:T(8,128)}, u32[]{:S(2)}) copy-start(f32[16,5376]{1,0:T(8,128)} %param.15) | copy-start | bytes 1032196
  10.4 37.3 %copy-start.6 = (f32[16,5376]{1,0:T(8,128)S(1)}, f32[16,5376]{1,0:T(8,128)}, u32[]{:S(2)}) copy-start(f32[16,5376]{1,0:T(8,128)} %param.13) | copy-start | bytes 1032196
  38.0 9.6 %all-to-all-start = ((bf16[8,2,5376]{2,1,0:T(2,128)(2,1)}), bf16[8,2,5376]{2,1,0:T(2,128)(2,1)S(1)}, u32[]{:S(2)}, u32[]{:S(2)}) async-start(bf16[8,2,5376]{2,1,0:T(2,128)(2,1)} %reshape.53), calls=%async_computation.1 | async-start | bytes 344064 | tf_op jit(solution)/shard_map/all_to_all | solution.py:56
  48.9 26.1 %copy-start.1 = (f32[16,5376]{1,0:T(8,128)}, f32[16,5376]{1,0:T(8,128)S(1)}, u32[]{:S(2)}) copy-start(f32[16,5376]{1,0:T(8,128)S(1)} %get-tuple-element.5) | copy-start | bytes 1032196
  48.9 26.1 %copy-start.2 = (s32[128]{0:T(128)S(1)}, s32[128]{0:T(128)}, u32[]{:S(2)}) copy-start(s32[128]{0:T(128)} %param.9) | copy-start | bytes 1540
Sparse Core Ops, SparseCore 0:
  10.9 25.2 reduce-scatter.1
where the time goes:
time: 83.8 us; the launch traced here: 83.5 us
  waiting for transfers between devices  31.3 us (37%)
  blocking collectives  25.4 us (30%)
  between operations  14.1 us (17%)
  matrix products  6.3 us (8%)
  starting transfers between devices  3.67 us (4%)
  local copies, waits for them, and re-layouts  2.41 us (3%)
    reduce_scatter x1, waiting for transfers between devices, on_device(): lax.psum_scatter(jnp.dot(selector, grads, preferred_element_type=jnp.floa...  25.4 us
    all_gather x1, blocking collectives, on_device(): shard_rows = lax.all_gather(listed_rows, 'local', axis=0, tiled=True)  17.1 us
    all_to_all x1, blocking collectives, on_device(): lax.all_to_all(reply_rows.reshape(node_count, capacity, width), 'node', s...  8.37 us
    all_to_all x1, waiting for transfers between devices, on_device(): lax.all_to_all(outgoing.reshape(node_count, capacity, width), 'node', spl...  5.95 us
    all_to_all x1, starting transfers between devices, on_device(): lax.all_to_all(outgoing.reshape(node_count, capacity, width), 'node', spl...  3.63 us
    dot_general x1, matrix products, on_device(): jnp.dot(selector, grads, preferred_element_type=jnp.float32)  1.84 us
  transfers between devices with their start and end apart: 2, of which 2 were waited for; matrix products, arithmetic and copies ran while one was open for 0% of the time, Pallas kernels for 0%

commit v1 on v0

v1 whole, which is shorter than its diff:
```python
import functools

import jax
import jax.numpy as jnp
from jax import lax
from jax.experimental import pallas as pl
from jax.experimental.pallas import tpu as pltpu
from jax.sharding import PartitionSpec as P

VOCAB = 262144
STEP = 100

BETA_ONE = 0.9
BETA_TWO = 0.999
LEARN_RATE = 0.01
EPSILON = 1e-08

MESH = pl.DeviceIdType.MESH
CHUNKS = 3
AHEAD = 2
BLOCKS = 7
TILE = 16
F32 = jnp.float32
BF16 = jnp.bfloat16


def adam_rows(gradient, moment, second, master, kept):
    corr_one = 1.0 - BETA_ONE**STEP
    corr_two = 1.0 - BETA_TWO**STEP
    moment_new = BETA_ONE * moment + (1.0 - BETA_ONE) * gradient
    second_new = BETA_TWO * second + (1.0 - BETA_TWO) * gradient * gradient
    master_new = master - LEARN_RATE * (moment_new / corr_one) / (
        jnp.sqrt(second_new / corr_two) + EPSILON
    )
    return (
        jnp.where(kept, moment_new, moment),
        jnp.where(kept, second_new, second),
        jnp.where(kept, master_new, master),
    )


def repeat(count, body):
    if count <= 8:
        for step in range(count):
            body(step)
    else:
        lax.fori_loop(0, count, lambda step, carry: (body(step), carry)[1], None)


def dot(a, b):
    return jnp.dot(a, b, preferred_element_type=F32)


def kernel(
    nodes,
    locals_,
    cap,
    slot_ref,
    ids_ref,
    touched_ref,
    omap_ref,
    grads_hbm,
    moment_hbm,
    second_hbm,
    master_hbm,
    tok_out,
    moment_out,
    second_out,
    master_out,
    grads,
    moment,
    second,
    master,
    route,
    route_t,
    collect,
    collect_t,
    select,
    select_t,
    part,
    up_src,
    up_dst,
    dn_src,
    dn_dst,
    fwd_src,
    fwd_dst,
    rep_src,
    rep_dst,
    gath,
    load_sem,
    adam_sem,
    up_ss,
    up_rs,
    dn_ss,
    dn_rs,
    fwd_ss,
    fwd_rs,
    rep_ss,
    rep_rs,
    ag_up_ss,
    ag_dn_ss,
    ag_rs,
):
    n = lax.axis_index("node")
    j = lax.axis_index("local")
    last = locals_ - 1
    width = grads.shape[1]
    cw = width // CHUNKS
    bw = cw // BLOCKS
    slots = part.shape[2]
    group = TILE // cap
    stacked = BLOCKS * slots

    loads = []
    for k in range(CHUNKS):
        cols = pl.ds(k * cw, cw)
        loads.append(
            pltpu.make_async_copy(grads_hbm.at[:, cols], grads.at[:, cols], load_sem.at[k])
        )
        loads[-1].start()
    adam_loads = [
        pltpu.make_async_copy(src, dst, adam_sem.at[i])
        for i, (src, dst) in enumerate(
            ((moment_hbm, moment), (second_hbm, second), (master_hbm, master))
        )
    ]
    for copy in adam_loads:
        copy.start()

    barrier = pltpu.get_barrier_semaphore()

    def greet(p):
        pl.semaphore_signal(
            barrier, inc=1, device_id=(lax.rem(n + p + 1, nodes), j), device_id_type=MESH
        )

    @pl.when(j > 0)
    def _():
        pl.semaphore_signal(barrier, inc=1, device_id=(n, j - 1), device_id_type=MESH)

    @pl.when(j < last)
    def _():
        pl.semaphore_signal(barrier, inc=1, device_id=(n, j + 1), device_id_type=MESH)

    repeat(nodes - 1, greet)

    def iota(shape, dim):
        return lax.broadcasted_iota(jnp.int32, shape, dim)

    shape = select.shape
    chosen = jnp.where(iota(shape, 0) == slot_ref[...], 1.0, 0.0).astype(F32)
    select[...] = chosen.astype(BF16)

    ids = ids_ref[...]
    rows_node = VOCAB // nodes
    owner = lax.shift_right_logical(ids, rows_node.bit_length() - 1).astype(F32)
    shape = (slots, stacked)
    sub, lane = iota(shape, 0), iota(shape, 1)
    owner_col = jnp.sum(jnp.where(lane == sub, owner, 0.0), axis=1, keepdims=True)
    earlier = (owner_col == owner) & (sub < lane % slots)
    rank = jnp.sum(jnp.where(earlier, 1.0, 0.0), axis=0, keepdims=True)
    sent = owner * float(cap) + rank
    shape = route.shape
    sub, lane = iota(shape, 0), iota(shape, 1)
    wanted = ((sub // TILE) * cap + (sub % TILE) // group).astype(F32)
    routed = jnp.where((wanted == sent) & (sub % group == lane // slots), 1.0, 0.0).astype(F32)
    route[...] = routed.astype(BF16)

    shape = collect.shape
    sub, lane = iota(shape, 0), iota(shape, 1)
    taken = jnp.where(
        (sub % TILE == omap_ref[...]) & (sub // TILE == lane % group), 1.0, 0.0
    ).astype(F32)
    collect[...] = taken.astype(BF16)

    touch = touched_ref[...].astype(F32)
    shape = (touch.shape[1], touch.shape[1])
    diagonal = iota(shape, 0) == iota(shape, 1)
    kept = jnp.sum(jnp.where(diagonal, touch, 0.0), axis=1, keepdims=True) >= 0.0

    line_peers = jnp.minimum(j, 1) + jnp.minimum(last - j, 1)
    pl.semaphore_wait(barrier, nodes - 1 + line_peers)

    def up_copy(k, s):
        return pltpu.make_async_remote_copy(
            up_src.at[k, s],
            up_dst.at[k, s],
            up_ss.at[k, s],
            up_rs.at[k, s],
            device_id=(n, jnp.minimum(j + 1, last)),
            device_id_type=MESH,
        )

    def dn_copy(k, s):
        return pltpu.make_async_remote_copy(
            dn_src.at[k, s],
            dn_dst.at[k, s],
            dn_ss.at[k, s],
            dn_rs.at[k, s],
            device_id=(n, jnp.maximum(j - 1, 0)),
            device_id_type=MESH,
        )

    def ag_copy(k, t, up):
        return pltpu.make_async_remote_copy(
            gath.at[k, t],
            gath.at[k, t],
            (ag_up_ss if up else ag_dn_ss).at[k, t],
            ag_rs.at[k, t],
            device_id=(n, jnp.minimum(j + 1, last) if up else jnp.maximum(j - 1, 0)),
            device_id_type=MESH,
        )

    def send_nodes(k, src, dst, ss, rs):
        def send(p):
            peer = lax.rem(n + p + 1, nodes)
            pltpu.make_async_remote_copy(
                src.at[k, peer],
                dst.at[k, n],
                ss.at[k],
                rs.at[k],
                device_id=(peer, j),
                device_id_type=MESH,
            ).start()

        repeat(nodes - 1, send)
        dst[k, n] = src[k, n]

    def wait_nodes(k, buf, sem):
        whole = buf.at[k, pl.ds(0, nodes - 1)]
        pltpu.make_async_copy(whole, whole, sem.at[k]).wait()

    def begin(k):
        loads[k].wait()
        sums = dot(select[...], grads[:, k * cw : (k + 1) * cw])
        part[k] = sums.reshape(locals_, slots, cw)

        @pl.when(j == 0)
        def _():
            def step(s):
                up_src[k, s] = part[k, last - s].astype(BF16)
                up_copy(k, s).start()

            repeat(last, step)

        @pl.when(j == last)
        def _():
            def step(s):
                dn_src[k, s] = part[k, s].astype(BF16)
                dn_copy(k, s).start()

            repeat(last, step)

    def relay(k):
        def step(s):
            t = last - s

            @pl.when((j > 0) & (t > j))
            def _():
                up_copy(k, s).wait_recv()
                up_src[k, s] = (up_dst[k, s].astype(F32) + part[k, t]).astype(BF16)
                up_copy(k, s).start()

            @pl.when((j < last) & (s < j))
            def _():
                dn_copy(k, s).wait_recv()
                dn_src[k, s] = (dn_dst[k, s].astype(F32) + part[k, s]).astype(BF16)
                dn_copy(k, s).start()

        repeat(last, step)

        @pl.when(j > 0)
        def _():
            up_copy(k, last - j).wait_recv()
            part[k, j] = part[k, j] + up_dst[k, last - j].astype(F32)

        @pl.when(j < last)
        def _():
            dn_copy(k, j).wait_recv()
            part[k, j] = part[k, j] + dn_dst[k, j].astype(F32)

        own = part[k, j].astype(BF16)
        tall = jnp.concatenate([own[:, b * bw : (b + 1) * bw] for b in range(BLOCKS)], axis=0)
        fwd_src[k] = dot(route[...], tall).astype(BF16).reshape(nodes, TILE, bw)
        send_nodes(k, fwd_src, fwd_dst, fwd_ss, fwd_rs)

    def update(k):
        if k == 0:
            for copy in adam_loads:
                copy.wait()
        wait_nodes(k, fwd_dst, fwd_rs)
        gradient = dot(collect[...], fwd_dst[k].reshape(nodes * TILE, bw))
        fresh = []
        for b in range(BLOCKS):
            cols = slice(k * cw + b * bw, k * cw + (b + 1) * bw)
            new = adam_rows(
                gradient[b * TILE : (b + 1) * TILE],
                moment[:, cols],
                second[:, cols],
                master[:, cols],
                kept,
            )
            moment_out[:, cols], second_out[:, cols], master_out[:, cols] = new
            fresh.append(new[2].astype(BF16))
        tall = jnp.concatenate(fresh, axis=0)
        rep_src[k] = dot(collect_t[...], tall).astype(BF16).reshape(nodes, TILE, bw)
        send_nodes(k, rep_src, rep_dst, rep_ss, rep_rs)

    def listed(k):
        wait_nodes(k, rep_dst, rep_rs)
        rows = dot(route_t[...], rep_dst[k].reshape(nodes * TILE, bw)).astype(BF16)
        for b in range(BLOCKS):
            gath[k, j, :, b * bw : (b + 1) * bw] = rows[b * slots : (b + 1) * slots]

        @pl.when(j < last)
        def _():
            ag_copy(k, j, True).start()

        @pl.when(j > 0)
        def _():
            ag_copy(k, j, False).start()

    def spread(k):
        def step(d):
            low, high = j - 1 - d, j + 1 + d

            @pl.when(low >= 0)
            def _():
                ag_copy(k, low, True).wait_recv()

                @pl.when(j < last)
                def _():
                    ag_copy(k, low, True).start()

            @pl.when(high <= last)
            def _():
                ag_copy(k, high, False).wait_recv()

                @pl.when(j > 0)
                def _():
                    ag_copy(k, high, False).start()

        repeat(last, step)
        rows = gath[k].reshape(locals_ * slots, cw)
        tok_out[:, k * cw : (k + 1) * cw] = dot(select_t[...], rows).astype(BF16)

    for k in range(min(AHEAD, CHUNKS)):
        begin(k)
    route_t[...] = routed.T.astype(BF16)
    collect_t[...] = taken.T.astype(BF16)
    select_t[...] = chosen.T.astype(BF16)
    for tick in range(CHUNKS + 3):
        if tick < CHUNKS:
            relay(tick)
        if tick + AHEAD < CHUNKS:
            begin(tick + AHEAD)
        if 0 <= tick - 1 < CHUNKS:
            update(tick - 1)
        if 0 <= tick - 2 < CHUNKS:
            listed(tick - 2)
        if 0 <= tick - 3 < CHUNKS:
            spread(tick - 3)

    for k in range(CHUNKS):
        wait_nodes(k, fwd_src, fwd_ss)
        wait_nodes(k, rep_src, rep_ss)

        def drain(s):
            @pl.when(last - s > j)
            def _():
                up_copy(k, s).wait_send()

            @pl.when(s < j)
            def _():
                dn_copy(k, s).wait_send()

        repeat(last, drain)

        def drain_gather(t):
            @pl.when((t <= j) & (j < last))
            def _():
                ag_copy(k, t, True).wait_send()

            @pl.when((t >= j) & (j > 0))
            def _():
                ag_copy(k, t, False).wait_send()

        repeat(locals_, drain_gather)


def on_device(nodes, locals_, grads, token_slot, node_ids, touched_ids, owner_map, moment, second, master):
    tokens, width = grads.shape
    slots = node_ids.shape[1]
    touch = touched_ids.shape[0]
    cap = owner_map.shape[2]
    group = TILE // cap
    cw = width // CHUNKS
    bw = cw // BLOCKS
    last = locals_ - 1
    vmem = pl.BlockSpec(memory_space=pltpu.VMEM)
    hbm = pl.BlockSpec(memory_space=pl.ANY)
    dma = pltpu.SemaphoreType.DMA
    outs = (
        jax.ShapeDtypeStruct((tokens, width), BF16),
        jax.ShapeDtypeStruct((touch, width), F32),
        jax.ShapeDtypeStruct((touch, width), F32),
        jax.ShapeDtypeStruct((touch, width), F32),
    )
    line = pltpu.VMEM((CHUNKS, last, slots, cw), BF16)
    plane = pltpu.VMEM((CHUNKS, nodes, TILE, bw), BF16)
    stacked = BLOCKS * slots
    return pl.pallas_call(
        functools.partial(kernel, nodes, locals_, cap),
        out_shape=outs,
        in_specs=[vmem] * 4 + [hbm] * 4,
        out_specs=[vmem] * 4,
        scratch_shapes=[
            pltpu.VMEM((tokens, width), BF16),
            pltpu.VMEM((touch, width), F32),
            pltpu.VMEM((touch, width), F32),
            pltpu.VMEM((touch, width), F32),
            pltpu.VMEM((nodes * TILE, stacked), BF16),
            pltpu.VMEM((stacked, nodes * TILE), BF16),
            pltpu.VMEM((BLOCKS * touch, nodes * TILE), BF16),
            pltpu.VMEM((nodes * TILE, BLOCKS * touch), BF16),
            pltpu.VMEM((locals_ * slots, tokens), BF16),
            pltpu.VMEM((tokens, locals_ * slots), BF16),
            pltpu.VMEM((CHUNKS, locals_, slots, cw), F32),
            line,
            line,
            line,
            line,
            plane,
            plane,
            plane,
            plane,
            pltpu.VMEM((CHUNKS, locals_, slots, cw), BF16),
            dma((CHUNKS,)),
            dma((3,)),
            dma((CHUNKS, last)),
            dma((CHUNKS, last)),
            dma((CHUNKS, last)),
            dma((CHUNKS, last)),
            dma((CHUNKS,)),
            dma((CHUNKS,)),
            dma((CHUNKS,)),
            dma((CHUNKS,)),
            dma((CHUNKS, locals_)),
            dma((CHUNKS, locals_)),
            dma((CHUNKS, locals_)),
        ],
        compiler_params=pltpu.CompilerParams(
            collective_id=0, has_side_effects=True, vmem_limit_bytes=56 * 1024 * 1024
        ),
    )(
        token_slot.reshape(1, tokens),
        jnp.tile(node_ids, (1, BLOCKS)),
        touched_ids.reshape(1, touch),
        jnp.repeat(owner_map.reshape(1, nodes * cap), group, axis=1),
        grads,
        moment,
        second,
        master,
    )


def solution(mesh):
    nodes, locals_ = mesh.shape["node"], mesh.shape["local"]
    placed = (
        P(("node", "local"), None),
        P(("node", "local")),
        P("node", "local"),
        P(("node", "local")),
        P(("node", "local"), None, None),
        P(("node", "local"), None),
        P(("node", "local"), None),
        P(("node", "local"), None),
    )
    return jax.shard_map(
        functools.partial(on_device, nodes, locals_),
        mesh=mesh,
        in_specs=placed,
        out_specs=(P(("node", "local"), None),) * 4,
        check_vma=False,
    )
```

time: 83.8 us -> 65.2 us (0.78)
  Pallas kernels: 0 us -> 56.8 us
  waiting for transfers between devices: 31.3 us -> 0 us
  blocking collectives: 25.4 us -> 0 us
  between operations: 14.1 us -> 0.66 us
  matrix products: 6.3 us -> 0 us
  local copies, waits for them, and re-layouts: 2.41 us -> 7.53 us
  starting transfers between devices: 3.67 us -> 0 us
    pallas_call x0 -> x1, Pallas kernels: none -> 56.8 us  [on_device(): pl.pallas_call(functools.partial(kernel, nodes, locals_, cap), out_shape=...]
    reduce_scatter x1 -> x0, waiting for transfers between devices: 25.4 us -> none  [on_device(): lax.psum_scatter(jnp.dot(selector, grads, preferred_element_type=jnp.floa...]
    all_gather x1 -> x0, blocking collectives: 17.1 us -> none  [on_device(): shard_rows = lax.all_gather(listed_rows, 'local', axis=0, tiled=True)]
    all_to_all x1 -> x0, blocking collectives: 8.37 us -> none  [on_device(): lax.all_to_all(reply_rows.reshape(node_count, capacity, width), 'node', s...]
    dot_general x6 -> x0, matrix products: 6.3 us -> none  [the longest x1 1.84 us: on_device(): jnp.dot(selector, grads, preferred_element_type=jnp.float32)]
    all_to_all x1 -> x0, waiting for transfers between devices: 5.95 us -> none  [on_device(): lax.all_to_all(outgoing.reshape(node_count, capacity, width), 'node', spl...]
    unnamed x19 -> x11, local copies, waits for them, and re-layouts: 1.38 us -> 5.52 us
    all_to_all x1 -> x0, starting transfers between devices: 3.63 us -> none  [on_device(): lax.all_to_all(outgoing.reshape(node_count, capacity, width), 'node', spl...]
  transfers between devices with their start and end apart: 2 -> 0, of which waited for: 2 -> 0; matrix products, arithmetic and copies ran while one was open for 0% -> 0% of each run, Pallas kernels for 0% -> 0%
where the time goes in v1:
time: 65.2 us; the launch traced here: 65 us
  Pallas kernels  56.8 us (87%)
  local copies, waits for them, and re-layouts  7.53 us (12%)
  between operations  0.66 us (1%)
    pallas_call x1, Pallas kernels, on_device(): pl.pallas_call(functools.partial(kernel, nodes, locals_, cap), out_shape=...  56.8 us
    unnamed x11, local copies, waits for them, and re-layouts  5.52 us

profile of v1, /device:TPU:0, one launch (start us, length us, event | category | flops | bytes accessed | tf_op | source)
XLA Modules:
  0.0 65.0 jit_solution(7077604494965159961)
XLA Ops:
  0.6 0.7 %tile.12 = s32[7,16]{1,0:T(8,128)S(1)} broadcast(s32[16]{0:T(128)} %bitcast.3), dimensions={1} | broadcast | bytes 512 | tf_op jit(solution)/shard_map/tile | solution.py:457
  1.3 0.6 tile.13.ids_ref
  1.9 0.8 %copy.13 = s32[1,8,2]{2,1,0:T(8,128)S(1)} copy(s32[1,8,2]{1,2,0:T(2,128)} %param.12) | data formatting | bytes 128 | tf_op args[4]
  2.6 0.1 reshape.31
  2.7 0.1 broadcast_in_dim.5
  2.8 0.6 broadcast_in_dim.6.omap_ref
  3.4 56.8 %shard_map.111 = (bf16[128,5376]{1,0:T(8,128)(2,1)}, f32[16,5376]{1,0:T(8,128)}, f32[16,5376]{1,0:T(8,128)}, f32[16,5376]{1,0:T(8,128)}) custom-call(s32[1,128]{1,0:T(1,128)} %bitcast.4, s32[1,112]{1,0:T(1,128)} %tile.13.ids_ref, s32[1,16]{1,0:T(1,128)} %bitcast.5, s32[1,128]{1,0:T(1,128)} %broadcast_in_dim.6.omap_ref, bf16[128,5376]{1,0:T(8,128)(2,1)} %grads_hbm.1, ...), custom_call_target="tpu_custom_call" | custom-call | tf_op jit(solution)/shard_map/pallas_call | solution.py:412
  60.3 0.0 copy-start.2
  60.3 0.0 copy-start.1
  60.3 2.6 %copy.18 = bf16[128,5376]{1,0:T(8,128)(2,1)} copy(bf16[128,5376]{1,0:T(8,128)(2,1)} %get-tuple-element.8) | data formatting | bytes 2752512
  62.8 0.0 copy-done.2
  62.8 0.0 copy-start
  62.8 0.7 %copy.19 = f32[16,5376]{1,0:T(8,128)} copy(f32[16,5376]{1,0:T(8,128)S(1)} %copy-done.2) | data formatting | bytes 688128
  63.6 0.0 copy-done.1
  63.6 0.7 %copy.20 = f32[16,5376]{1,0:T(8,128)} copy(f32[16,5376]{1,0:T(8,128)S(1)} %copy-done.1) | data formatting | bytes 688128
  64.3 0.0 copy-done
  64.3 0.7 %copy.21 = f32[16,5376]{1,0:T(8,128)} copy(f32[16,5376]{1,0:T(8,128)S(1)} %copy-done) | data formatting | bytes 688128
Async XLA Ops:
  60.3 2.6 %copy-start.2 = (f32[16,5376]{1,0:T(8,128)S(1)}, f32[16,5376]{1,0:T(8,128)}, u32[]{:S(2)}) copy-start(f32[16,5376]{1,0:T(8,128)} %get-tuple-element.9) | copy-start | bytes 1032196
  60.3 3.3 %copy-start.1 = (f32[16,5376]{1,0:T(8,128)S(1)}, f32[16,5376]{1,0:T(8,128)}, u32[]{:S(2)}) copy-start(f32[16,5376]{1,0:T(8,128)} %get-tuple-element.10) | copy-start | bytes 1032196
  62.8 1.5 %copy-start = (f32[16,5376]{1,0:T(8,128)S(1)}, f32[16,5376]{1,0:T(8,128)}, u32[]{:S(2)}) copy-start(f32[16,5376]{1,0:T(8,128)} %get-tuple-element.11) | copy-start | bytes 1032196

commit v2 on v1

--- a/solution.py
+++ b/solution.py
@@ -17,7 +17,6 @@
 
 MESH = pl.DeviceIdType.MESH
 CHUNKS = 3
-AHEAD = 2
 BLOCKS = 7
 TILE = 16
 F32 = jnp.float32
@@ -63,10 +62,8 @@
     moment_hbm,
     second_hbm,
     master_hbm,
-    tok_out,
-    moment_out,
-    second_out,
-    master_out,
+    gath,
+    gradient_out,
     grads,
     moment,
     second,
@@ -76,7 +73,6 @@
     collect,
     collect_t,
     select,
-    select_t,
     part,
     up_src,
     up_dst,
@@ -86,7 +82,6 @@
     fwd_dst,
     rep_src,
     rep_dst,
-    gath,
     load_sem,
     adam_sem,
     up_ss,
@@ -104,6 +99,7 @@
     n = lax.axis_index("node")
     j = lax.axis_index("local")
     last = locals_ - 1
+    half = locals_ // 2
     width = grads.shape[1]
     cw = width // CHUNKS
     bw = cw // BLOCKS
@@ -147,36 +143,44 @@
     def iota(shape, dim):
         return lax.broadcasted_iota(jnp.int32, shape, dim)
 
+    def column(row, size):
+        diagonal = iota((size, size), 0) == iota((size, size), 1)
+        return jnp.sum(jnp.where(diagonal, row, 0.0), axis=1, keepdims=True)
+
     shape = select.shape
-    chosen = jnp.where(iota(shape, 0) == slot_ref[...], 1.0, 0.0).astype(F32)
-    select[...] = chosen.astype(BF16)
-
-    ids = ids_ref[...]
+    select[...] = jnp.where(iota(shape, 0) == slot_ref[...], 1.0, 0.0).astype(BF16)
+
     rows_node = VOCAB // nodes
-    owner = lax.shift_right_logical(ids, rows_node.bit_length() - 1).astype(F32)
+    owner = lax.shift_right_logical(ids_ref[...], rows_node.bit_length() - 1).astype(F32)
+    shape = (slots, slots)
+    earlier = (column(owner, slots) == owner) & (iota(shape, 0) < iota(shape, 1))
+    rank = jnp.sum(jnp.where(earlier, 1.0, 0.0), axis=0, keepdims=True)
+    sent = column(owner * float(cap) + rank, slots)
     shape = (slots, stacked)
-    sub, lane = iota(shape, 0), iota(shape, 1)
-    owner_col = jnp.sum(jnp.where(lane == sub, owner, 0.0), axis=1, keepdims=True)
-    earlier = (owner_col == owner) & (sub < lane % slots)
-    rank = jnp.sum(jnp.where(earlier, 1.0, 0.0), axis=0, keepdims=True)
-    sent = owner * float(cap) + rank
+    sent = jnp.sum(
+        jnp.where(iota(shape, 0) == iota(shape, 1) % slots, sent, 0.0), axis=0, keepdims=True
+    )
     shape = route.shape
     sub, lane = iota(shape, 0), iota(shape, 1)
     wanted = ((sub // TILE) * cap + (sub % TILE) // group).astype(F32)
     routed = jnp.where((wanted == sent) & (sub % group == lane // slots), 1.0, 0.0).astype(F32)
     route[...] = routed.astype(BF16)
 
+    shape = (nodes, nodes * TILE)
+    sub, lane = iota(shape, 0), iota(shape, 1)
+    place = jnp.zeros((1, nodes * TILE), F32)
+    for c in range(cap):
+        held = column(omap_ref[c : c + 1, :].astype(F32), nodes)
+        here = (sub == lane // TILE) & ((lane % TILE) // group == c)
+        place = place + jnp.sum(jnp.where(here, held, 0.0), axis=0, keepdims=True)
     shape = collect.shape
     sub, lane = iota(shape, 0), iota(shape, 1)
     taken = jnp.where(
-        (sub % TILE == omap_ref[...]) & (sub // TILE == lane % group), 1.0, 0.0
+        ((sub % TILE).astype(F32) == place) & (sub // TILE == lane % group), 1.0, 0.0
     ).astype(F32)
     collect[...] = taken.astype(BF16)
 
-    touch = touched_ref[...].astype(F32)
-    shape = (touch.shape[1], touch.shape[1])
-    diagonal = iota(shape, 0) == iota(shape, 1)
-    kept = jnp.sum(jnp.where(diagonal, touch, 0.0), axis=1, keepdims=True) >= 0.0
+    kept = column(touched_ref[...].astype(F32), touched_ref.shape[1]) >= 0.0
 
     line_peers = jnp.minimum(j, 1) + jnp.minimum(last - j, 1)
     pl.semaphore_wait(barrier, nodes - 1 + line_peers)
@@ -202,9 +206,10 @@
         )
 
     def ag_copy(k, t, up):
+        rows = gath.at[pl.ds(pl.multiple_of(t * slots, slots), slots), pl.ds(k * cw, cw)]
         return pltpu.make_async_remote_copy(
-            gath.at[k, t],
-            gath.at[k, t],
+            rows,
+            rows,
             (ag_up_ss if up else ag_dn_ss).at[k, t],
             ag_rs.at[k, t],
             device_id=(n, jnp.minimum(j + 1, last) if up else jnp.maximum(j - 1, 0)),
@@ -251,17 +256,19 @@
 
             repeat(last, step)
 
-    def relay(k):
+    def up_relay(k):
         def step(s):
-            t = last - s
-
-            @pl.when((j > 0) & (t > j))
+            @pl.when(last - s > j)
             def _():
                 up_copy(k, s).wait_recv()
-                up_src[k, s] = (up_dst[k, s].astype(F32) + part[k, t]).astype(BF16)
+                up_src[k, s] = (up_dst[k, s].astype(F32) + part[k, last - s]).astype(BF16)
                 up_copy(k, s).start()
 
-            @pl.when((j < last) & (s < j))
+        repeat(last, step)
+
+    def dn_relay(k):
+        def step(s):
+            @pl.when(s < j)
             def _():
                 dn_copy(k, s).wait_recv()
                 dn_src[k, s] = (dn_dst[k, s].astype(F32) + part[k, s]).astype(BF16)
@@ -269,6 +276,15 @@
 
         repeat(last, step)
 
+    def near(k):
+        pl.when((j > 0) & (j < half))(lambda: up_relay(k))
+        pl.when((j < last) & (j >= half))(lambda: dn_relay(k))
+
+    def far(k):
+        pl.when((j > 0) & (j < half))(lambda: dn_relay(k))
+        pl.when((j < last) & (j >= half))(lambda: up_relay(k))
+
+    def forward(k):
         @pl.when(j > 0)
         def _():
             up_copy(k, last - j).wait_recv()
@@ -300,7 +316,7 @@
                 master[:, cols],
                 kept,
             )
-            moment_out[:, cols], second_out[:, cols], master_out[:, cols] = new
+            gradient_out[:, cols] = gradient[b * TILE : (b + 1) * TILE]
             fresh.append(new[2].astype(BF16))
         tall = jnp.concatenate(fresh, axis=0)
         rep_src[k] = dot(collect_t[...], tall).astype(BF16).reshape(nodes, TILE, bw)
@@ -309,8 +325,10 @@
     def listed(k):
         wait_nodes(k, rep_dst, rep_rs)
         rows = dot(route_t[...], rep_dst[k].reshape(nodes * TILE, bw)).astype(BF16)
+        own = pl.ds(pl.multiple_of(j * slots, slots), slots)
         for b in range(BLOCKS):
-            gath[k, j, :, b * bw : (b + 1) * bw] = rows[b * slots : (b + 1) * slots]
+            cols = slice(k * cw + b * bw, k * cw + (b + 1) * bw)
+            gath[own, cols] = rows[b * slots : (b + 1) * slots]
 
         @pl.when(j < last)
         def _():
@@ -320,46 +338,43 @@
         def _():
             ag_copy(k, j, False).start()
 
-    def spread(k):
-        def step(d):
-            low, high = j - 1 - d, j + 1 + d
-
-            @pl.when(low >= 0)
-            def _():
-                ag_copy(k, low, True).wait_recv()
-
-                @pl.when(j < last)
-                def _():
-                    ag_copy(k, low, True).start()
-
-            @pl.when(high <= last)
-            def _():
-                ag_copy(k, high, False).wait_recv()
-
-                @pl.when(j > 0)
-                def _():
-                    ag_copy(k, high, False).start()
-
-        repeat(last, step)
-        rows = gath[k].reshape(locals_ * slots, cw)
-        tok_out[:, k * cw : (k + 1) * cw] = dot(select_t[...], rows).astype(BF16)
-
-    for k in range(min(AHEAD, CHUNKS)):
+    def pass_on(k, d):
+        low, high = j - 1 - d, j + 1 + d
+
+        @pl.when(low >= 0)
+        def _():
+            ag_copy(k, low, True).wait_recv()
+
+            @pl.when(j < last)
+            def _():
+                ag_copy(k, low, True).start()
+
+        @pl.when(high <= last)
+        def _():
+            ag_copy(k, high, False).wait_recv()
+
+            @pl.when(j > 0)
+            def _():
+                ag_copy(k, high, False).start()
+
+    def first_hop(k):
+        pass_on(k, 0)
+
+    def middle_hops(k):
+        repeat(last - 2, lambda d: pass_on(k, d + 1))
+
+    def last_hop(k):
+        pass_on(k, last - 1)
+
+    for k in range(CHUNKS):
         begin(k)
     route_t[...] = routed.T.astype(BF16)
     collect_t[...] = taken.T.astype(BF16)
-    select_t[...] = chosen.T.astype(BF16)
-    for tick in range(CHUNKS + 3):
-        if tick < CHUNKS:
-            relay(tick)
-        if tick + AHEAD < CHUNKS:
-            begin(tick + AHEAD)
-        if 0 <= tick - 1 < CHUNKS:
-            update(tick - 1)
-        if 0 <= tick - 2 < CHUNKS:
-            listed(tick - 2)
-        if 0 <= tick - 3 < CHUNKS:
-            spread(tick - 3)
+    stages = (near, far, forward, update, listed, first_hop, middle_hops, last_hop)
+    for tick in range(CHUNKS + len(stages) - 1):
+        for depth in reversed(range(len(stages))):
+            if 0 <= tick - depth < CHUNKS:
+                stages[depth](tick - depth)
 
     for k in range(CHUNKS):
         wait_nodes(k, fwd_src, fwd_ss)
@@ -398,22 +413,20 @@
     bw = cw // BLOCKS
     last = locals_ - 1
     vmem = pl.BlockSpec(memory_space=pltpu.VMEM)
-    hbm = pl.BlockSpec(memory_space=pl.ANY)
+    hbm = pl.BlockSpec(memory_space=pltpu.HBM)
     dma = pltpu.SemaphoreType.DMA
-    outs = (
-        jax.ShapeDtypeStruct((tokens, width), BF16),
-        jax.ShapeDtypeStruct((touch, width), F32),
-        jax.ShapeDtypeStruct((touch, width), F32),
-        jax.ShapeDtypeStruct((touch, width), F32),
-    )
+    list_len = locals_ * slots
     line = pltpu.VMEM((CHUNKS, last, slots, cw), BF16)
     plane = pltpu.VMEM((CHUNKS, nodes, TILE, bw), BF16)
     stacked = BLOCKS * slots
-    return pl.pallas_call(
+    rows, gradient = pl.pallas_call(
         functools.partial(kernel, nodes, locals_, cap),
-        out_shape=outs,
+        out_shape=(
+            jax.ShapeDtypeStruct((list_len, width), BF16),
+            jax.ShapeDtypeStruct((touch, width), F32),
+        ),
         in_specs=[vmem] * 4 + [hbm] * 4,
-        out_specs=[vmem] * 4,
+        out_specs=[vmem] * 2,
         scratch_shapes=[
             pltpu.VMEM((tokens, width), BF16),
             pltpu.VMEM((touch, width), F32),
@@ -423,8 +436,7 @@
             pltpu.VMEM((stacked, nodes * TILE), BF16),
             pltpu.VMEM((BLOCKS * touch, nodes * TILE), BF16),
             pltpu.VMEM((nodes * TILE, BLOCKS * touch), BF16),
-            pltpu.VMEM((locals_ * slots, tokens), BF16),
-            pltpu.VMEM((tokens, locals_ * slots), BF16),
+            pltpu.VMEM((list_len, tokens), BF16),
             pltpu.VMEM((CHUNKS, locals_, slots, cw), F32),
             line,
             line,
@@ -434,7 +446,6 @@
             plane,
             plane,
             plane,
-            pltpu.VMEM((CHUNKS, locals_, slots, cw), BF16),
             dma((CHUNKS,)),
             dma((3,)),
             dma((CHUNKS, last)),
@@ -450,18 +461,24 @@
             dma((CHUNKS, locals_)),
         ],
         compiler_params=pltpu.CompilerParams(
-            collective_id=0, has_side_effects=True, vmem_limit_bytes=56 * 1024 * 1024
+            collective_id=0, has_side_effects=True, vmem_limit_bytes=44 * 1024 * 1024
         ),
     )(
         token_slot.reshape(1, tokens),
-        jnp.tile(node_ids, (1, BLOCKS)),
+        node_ids,
         touched_ids.reshape(1, touch),
-        jnp.repeat(owner_map.reshape(1, nodes * cap), group, axis=1),
+        jnp.swapaxes(owner_map, 1, 2).reshape(cap, nodes),
         grads,
         moment,
         second,
         master,
     )
+    moment_out, second_out, master_out = adam_rows(
+        gradient, moment, second, master, touched_ids[:, None] >= 0
+    )
+    wanted = lax.iota(jnp.int32, list_len)
+    selector = (token_slot[:, None] == wanted[None, :]).astype(BF16)
+    return dot(selector, rows).astype(BF16), moment_out, second_out, master_out
 
 
 def solution(mesh):

time: 65.2 us -> 53.1 us (0.81)
  Pallas kernels: 56.8 us -> 41.8 us
  other arithmetic: 0 us -> 1.8 us
  matrix products: 0 us -> 1.64 us
    pallas_call x1, Pallas kernels: 56.8 us -> 41.8 us  [on_device(): pl.pallas_call(functools.partial(kernel, nodes, locals_, cap), out_shape=...]
    dot_general x0 -> x1, matrix products: none -> 1.64 us  [dot(): return jnp.dot(a, b, preferred_element_type=F32)]
    unnamed x11 -> x16, local copies, waits for them, and re-layouts: 5.52 us -> 6.91 us
    another operation x2 -> x0, local copies, waits for them, and re-layouts: 1.25 us -> none  [on_device(): jnp.tile(node_ids, (1, BLOCKS))]
    select_n x0 -> x1, other arithmetic: none -> 1.14 us  [adam_rows(): jnp.where(kept, master_new, master)]
    broadcast_in_dim x2 -> x0, local copies, waits for them, and re-layouts: 0.68 us -> none  [on_device(): jnp.repeat(owner_map.reshape(1, nodes * cap), group, axis=1)]
    ge x0 -> x1, other arithmetic: none -> 0.66 us  [on_device(): touched_ids[:, None] >= 0]
where the time goes in v2:
time: 53.1 us; the launch traced here: 52.8 us
  Pallas kernels  41.8 us (79%)
  local copies, waits for them, and re-layouts  6.91 us (13%)
  other arithmetic  1.8 us (3%)
  matrix products  1.64 us (3%)
  between operations  0.65 us (1%)
    pallas_call x1, Pallas kernels, on_device(): pl.pallas_call(functools.partial(kernel, nodes, locals_, cap), out_shape=...  41.8 us
    unnamed x16, local copies, waits for them, and re-layouts  6.91 us
    dot_general x1, matrix products, dot(): return jnp.dot(a, b, preferred_element_type=F32)  1.64 us
    select_n x1, other arithmetic, adam_rows(): jnp.where(kept, master_new, master)  1.14 us

profile of v2, /device:TPU:0, one launch (start us, length us, event | category | flops | bytes accessed | tf_op | source)
XLA Modules:
  0.0 52.8 jit_solution(3924395491289591258)
XLA Ops:
  0.6 0.7 %broadcast_compare_fusion = pred[16]{0:T(512)(128)(4,1)S(1)} fusion(s32[16]{0:T(128)} %param.11), kind=kLoop, calls=%fused_computation.9 | loop fusion | flops 16 | bytes 80 | tf_op jit(solution)/shard_map/ge | solution.py:477
  1.3 0.0 copy-start
  1.3 1.0 %copy-done = f32[16,5376]{1,0:T(8,128)S(1)} copy-done((f32[16,5376]{1,0:T(8,128)S(1)}, f32[16,5376]{1,0:T(8,128)}, u32[]{:S(2)}) %copy-start) | copy-done | bytes 344088
  2.3 0.0 copy-start.1
  2.3 1.0 %copy-done.1 = f32[16,5376]{1,0:T(8,128)S(1)} copy-done((f32[16,5376]{1,0:T(8,128)S(1)}, f32[16,5376]{1,0:T(8,128)}, u32[]{:S(2)}) %copy-start.1) | copy-done | bytes 344088
  3.2 0.0 copy-start.2
  3.3 1.0 %copy-done.2 = f32[16,5376]{1,0:T(8,128)S(1)} copy-done((f32[16,5376]{1,0:T(8,128)S(1)}, f32[16,5376]{1,0:T(8,128)}, u32[]{:S(2)}) %copy-start.2) | copy-done | bytes 344088
  4.2 0.0 copy-start.3
  4.2 1.3 %copy-done.3 = bf16[128,5376]{1,0:T(8,128)(2,1)S(1)} copy-done((bf16[128,5376]{1,0:T(8,128)(2,1)S(1)}, bf16[128,5376]{1,0:T(8,128)(2,1)}, u32[]{:S(2)}) %copy-start.3) | copy-done | bytes 1376280
  5.6 0.0 copy-start.4
  5.6 0.7 %copy-done.4 = s32[128]{0:T(128)S(1)} copy-done((s32[128]{0:T(128)S(1)}, s32[128]{0:T(128)}, u32[]{:S(2)}) %copy-start.4) | copy-done | bytes 536
  6.2 0.0 copy-start.5
  6.2 0.7 %copy-done.5 = s32[1,8,2]{1,2,0:T(2,128)S(1)} copy-done((s32[1,8,2]{1,2,0:T(2,128)S(1)}, s32[1,8,2]{1,2,0:T(2,128)}, u32[]{:S(2)}) %copy-start.5) | copy-done | bytes 88
  6.9 0.0 copy-start.6
  6.9 0.7 %copy-done.6 = s32[1,16]{1,0:T(1,128)S(1)} copy-done((s32[1,16]{1,0:T(1,128)S(1)}, s32[1,16]{1,0:T(1,128)}, u32[]{:S(2)}) %copy-start.6) | copy-done | bytes 88
  7.6 0.0 copy-start.7
  7.6 0.7 %copy-done.7 = s32[16]{0:T(128)S(1)} copy-done((s32[16]{0:T(128)S(1)}, s32[16]{0:T(128)}, u32[]{:S(2)}) %copy-start.7) | copy-done | bytes 88
  8.2 41.8 %shard_map.111 = (bf16[64,5376]{1,0:T(8,128)(2,1)S(1)}, f32[16,5376]{1,0:T(8,128)S(1)}) custom-call(s32[1,128]{1,0:T(1,128)S(1)} %bitcast.6, s32[1,16]{1,0:T(1,128)S(1)} %copy-done.6, s32[1,16]{1,0:T(1,128)S(1)} %bitcast.8, s32[2,8]{1,0:T(2,128)S(1)} %bitcast.7, bf16[128,5376]{1,0:T(8,128)(2,1)S(1)} %copy-done.3, f32[16,5376]{1,0:T(8,128)S(1)} %copy-done, ...), custom_call_target="tpu_custom_call" | custom-call | tf_op jit(solution)/shard_map/pallas_call | solution.py:422
  50.0 1.6 %convolution_convert_fusion = bf16[128,5376]{1,0:T(8,128)(2,1)} fusion(bf16[64,5376]{1,0:T(8,128)(2,1)S(1)} %get-tuple-element.6, s32[128]{0:T(128)S(1)} %copy-done.4), kind=kOutput, calls=%fused_computation | convolution fusion | flops 88776704 | bytes 2064896 | tf_op jit(solution)/shard_map/dot_general | solution.py:50
  51.6 1.1 %subtract_select_fusion = (f32[16,5376]{1,0:T(8,128)}, f32[16,5376]{1,0:T(8,128)}, f32[16,5376]{1,0:T(8,128)}) fusion(f32[16,5376]{1,0:T(8,128)S(1)} %copy-done.2, f32[16,5376]{1,0:T(8,128)S(1)} %get-tuple-element.7, f32[16,5376]{1,0:T(8,128)S(1)} %copy-done, f32[16,5376]{1,0:T(8,128)S(1)} %copy-done.1, pred[16]{0:T(512)(128)(4,1)S(1)} %broadcast_compare_fusion), kind=kLoop, calls=%fused_computation.1 | loop fusion | flops 1290240 | bytes 2408464 | tf_op jit(solution)/shard_map/jit(_where)/select_n | solution.py:37
Async XLA Ops:
  1.3 1.0 %copy-start = (f32[16,5376]{1,0:T(8,128)S(1)}, f32[16,5376]{1,0:T(8,128)}, u32[]{:S(2)}) copy-start(f32[16,5376]{1,0:T(8,128)} %moment_hbm.1) | copy-start | bytes 1032196
  2.3 1.0 %copy-start.1 = (f32[16,5376]{1,0:T(8,128)S(1)}, f32[16,5376]{1,0:T(8,128)}, u32[]{:S(2)}) copy-start(f32[16,5376]{1,0:T(8,128)} %second_hbm.1) | copy-start | bytes 1032196
  3.2 1.0 %copy-start.2 = (f32[16,5376]{1,0:T(8,128)S(1)}, f32[16,5376]{1,0:T(8,128)}, u32[]{:S(2)}) copy-start(f32[16,5376]{1,0:T(8,128)} %master_hbm.1) | copy-start | bytes 1032196
  4.2 1.3 %copy-start.3 = (bf16[128,5376]{1,0:T(8,128)(2,1)S(1)}, bf16[128,5376]{1,0:T(8,128)(2,1)}, u32[]{:S(2)}) copy-start(bf16[128,5376]{1,0:T(8,128)(2,1)} %grads_hbm.1) | copy-start | bytes 4128772
  5.6 0.7 %copy-start.4 = (s32[128]{0:T(128)S(1)}, s32[128]{0:T(128)}, u32[]{:S(2)}) copy-start(s32[128]{0:T(128)} %param.9) | copy-start | bytes 1540
  6.2 0.7 %copy-start.5 = (s32[1,8,2]{1,2,0:T(2,128)S(1)}, s32[1,8,2]{1,2,0:T(2,128)}, u32[]{:S(2)}) copy-start(s32[1,8,2]{1,2,0:T(2,128)} %param.12) | copy-start | bytes 196
  6.9 0.7 %copy-start.6 = (s32[1,16]{1,0:T(1,128)S(1)}, s32[1,16]{1,0:T(1,128)}, u32[]{:S(2)}) copy-start(s32[1,16]{1,0:T(1,128)} %ids_ref.1) | copy-start | bytes 196
  7.6 0.7 %copy-start.7 = (s32[16]{0:T(128)S(1)}, s32[16]{0:T(128)}, u32[]{:S(2)}) copy-start(s32[16]{0:T(128)} %param.11) | copy-start | bytes 196

commit v3 on v2

--- a/solution.py
+++ b/solution.py
@@ -44,6 +44,14 @@
             body(step)
     else:
         lax.fori_loop(0, count, lambda step, carry: (body(step), carry)[1], None)
+
+
+def div(x, m):
+    return lax.shift_right_logical(x, m.bit_length() - 1) if m & (m - 1) == 0 else x // m
+
+
+def mod(x, m):
+    return x & (m - 1) if m & (m - 1) == 0 else x % m
 
 
 def dot(a, b):
@@ -130,14 +138,24 @@
             barrier, inc=1, device_id=(lax.rem(n + p + 1, nodes), j), device_id_type=MESH
         )
 
-    @pl.when(j > 0)
-    def _():
-        pl.semaphore_signal(barrier, inc=1, device_id=(n, j - 1), device_id_type=MESH)
-
-    @pl.when(j < last)
-    def _():
-        pl.semaphore_signal(barrier, inc=1, device_id=(n, j + 1), device_id_type=MESH)
-
+    def greet_line(peer):
+        pl.semaphore_signal(barrier, inc=1, device_id=(n, peer), device_id_type=MESH)
+
+    tree = locals_ == 4
+    inner = jnp.clip(j, 1, 2)
+    outer = 3 * (inner - 1)
+    far_inner, far_outer = 3 - inner, 3 - outer
+    partner = inner + outer - j
+    is_inner = j == inner
+    if tree:
+        greet_line(partner)
+        greet_line(far_inner)
+        pl.when(is_inner)(lambda: greet_line(far_outer))
+        line_peers = 2 + jnp.minimum(j, 1) * jnp.minimum(last - j, 1)
+    else:
+        pl.when(j > 0)(lambda: greet_line(j - 1))
+        pl.when(j < last)(lambda: greet_line(j + 1))
+        line_peers = jnp.minimum(j, 1) + jnp.minimum(last - j, 1)
     repeat(nodes - 1, greet)
 
     def iota(shape, dim):
@@ -150,39 +168,6 @@
     shape = select.shape
     select[...] = jnp.where(iota(shape, 0) == slot_ref[...], 1.0, 0.0).astype(BF16)
 
-    rows_node = VOCAB // nodes
-    owner = lax.shift_right_logical(ids_ref[...], rows_node.bit_length() - 1).astype(F32)
-    shape = (slots, slots)
-    earlier = (column(owner, slots) == owner) & (iota(shape, 0) < iota(shape, 1))
-    rank = jnp.sum(jnp.where(earlier, 1.0, 0.0), axis=0, keepdims=True)
-    sent = column(owner * float(cap) + rank, slots)
-    shape = (slots, stacked)
-    sent = jnp.sum(
-        jnp.where(iota(shape, 0) == iota(shape, 1) % slots, sent, 0.0), axis=0, keepdims=True
-    )
-    shape = route.shape
-    sub, lane = iota(shape, 0), iota(shape, 1)
-    wanted = ((sub // TILE) * cap + (sub % TILE) // group).astype(F32)
-    routed = jnp.where((wanted == sent) & (sub % group == lane // slots), 1.0, 0.0).astype(F32)
-    route[...] = routed.astype(BF16)
-
-    shape = (nodes, nodes * TILE)
-    sub, lane = iota(shape, 0), iota(shape, 1)
-    place = jnp.zeros((1, nodes * TILE), F32)
-    for c in range(cap):
-        held = column(omap_ref[c : c + 1, :].astype(F32), nodes)
-        here = (sub == lane // TILE) & ((lane % TILE) // group == c)
-        place = place + jnp.sum(jnp.where(here, held, 0.0), axis=0, keepdims=True)
-    shape = collect.shape
-    sub, lane = iota(shape, 0), iota(shape, 1)
-    taken = jnp.where(
-        ((sub % TILE).astype(F32) == place) & (sub // TILE == lane % group), 1.0, 0.0
-    ).astype(F32)
-    collect[...] = taken.astype(BF16)
-
-    kept = column(touched_ref[...].astype(F32), touched_ref.shape[1]) >= 0.0
-
-    line_peers = jnp.minimum(j, 1) + jnp.minimum(last - j, 1)
     pl.semaphore_wait(barrier, nodes - 1 + line_peers)
 
     def up_copy(k, s):
@@ -235,10 +220,13 @@
         whole = buf.at[k, pl.ds(0, nodes - 1)]
         pltpu.make_async_copy(whole, whole, sem.at[k]).wait()
 
+    def sums(k):
+        loads[k].wait()
+        total = dot(select[...], grads[:, k * cw : (k + 1) * cw])
+        part[k] = total.reshape(locals_, slots, cw)
+
     def begin(k):
-        loads[k].wait()
-        sums = dot(select[...], grads[:, k * cw : (k + 1) * cw])
-        part[k] = sums.reshape(locals_, slots, cw)
+        sums(k)
 
         @pl.when(j == 0)
         def _():
@@ -295,7 +283,10 @@
             dn_copy(k, j).wait_recv()
             part[k, j] = part[k, j] + dn_dst[k, j].astype(F32)
 
-        own = part[k, j].astype(BF16)
+        send_out(k, part[k, j])
+
+    def send_out(k, total):
+        own = total.astype(BF16)
         tall = jnp.concatenate([own[:, b * bw : (b + 1) * bw] for b in range(BLOCKS)], axis=0)
         fwd_src[k] = dot(route[...], tall).astype(BF16).reshape(nodes, TILE, bw)
         send_nodes(k, fwd_src, fwd_dst, fwd_ss, fwd_rs)
@@ -322,7 +313,7 @@
         rep_src[k] = dot(collect_t[...], tall).astype(BF16).reshape(nodes, TILE, bw)
         send_nodes(k, rep_src, rep_dst, rep_ss, rep_rs)
 
-    def listed(k):
+    def fill(k):
         wait_nodes(k, rep_dst, rep_rs)
         rows = dot(route_t[...], rep_dst[k].reshape(nodes * TILE, bw)).astype(BF16)
         own = pl.ds(pl.multiple_of(j * slots, slots), slots)
@@ -330,6 +321,9 @@
             cols = slice(k * cw + b * bw, k * cw + (b + 1) * bw)
             gath[own, cols] = rows[b * slots : (b + 1) * slots]
 
+    def listed(k):
+        fill(k)
+
         @pl.when(j < last)
         def _():
             ag_copy(k, j, True).start()
@@ -366,11 +360,149 @@
     def last_hop(k):
         pass_on(k, last - 1)
 
+    def pair_copy(k):
+        rows = pl.ds(0, 2)
+        return pltpu.make_async_remote_copy(
+            up_src.at[k, rows],
+            up_dst.at[k, rows],
+            up_ss.at[k, 0],
+            up_rs.at[k, 0],
+            device_id=(n, partner),
+            device_id_type=MESH,
+        )
+
+    def partner_copy(k):
+        return pltpu.make_async_remote_copy(
+            up_src.at[k, 2],
+            up_dst.at[k, 2],
+            up_ss.at[k, 2],
+            up_rs.at[k, 1],
+            device_id=(n, partner),
+            device_id_type=MESH,
+        )
+
+    def far_copy(k, i):
+        return pltpu.make_async_remote_copy(
+            up_src.at[k, i],
+            dn_dst.at[k, 0],
+            up_ss.at[k, i],
+            up_rs.at[k, 2],
+            device_id=(n, far_outer if i else far_inner),
+            device_id_type=MESH,
+        )
+
+    def row_copy(k, t, peer, i):
+        rows = gath.at[pl.ds(pl.multiple_of(t * slots, slots), slots), pl.ds(k * cw, cw)]
+        return pltpu.make_async_remote_copy(
+            rows,
+            rows,
+            ag_up_ss.at[k, i],
+            ag_rs.at[k, t],
+            device_id=(n, peer),
+            device_id_type=MESH,
+        )
+
+    def tree_begin(k):
+        sums(k)
+
+        @pl.when(~is_inner)
+        def _():
+            up_src[k, 0] = part[k, far_inner].astype(BF16)
+            up_src[k, 1] = part[k, far_outer].astype(BF16)
+            pair_copy(k).start()
+
+        up_src[k, 2] = part[k, partner].astype(BF16)
+        partner_copy(k).start()
+
+    def merge(k):
+        @pl.when(is_inner)
+        def _():
+            pair_copy(k).wait_recv()
+            for i, t in enumerate((far_inner, far_outer)):
+                up_src[k, i] = (up_dst[k, i].astype(F32) + part[k, t]).astype(BF16)
+                far_copy(k, i).start()
+
+    def tree_forward(k):
+        partner_copy(k).wait_recv()
+        far_copy(k, 0).wait_recv()
+        send_out(k, part[k, j] + up_dst[k, 2].astype(F32) + dn_dst[k, 0].astype(F32))
+
+    def tree_listed(k):
+        fill(k)
+        row_copy(k, j, far_inner, 0).start()
+        row_copy(k, j, partner, 1).start()
+
+    def tree_pass(k):
+        @pl.when(is_inner)
+        def _():
+            for i, t in enumerate((far_inner, far_outer)):
+                row_copy(k, t, partner, 2 + i).wait_recv()
+                row_copy(k, t, partner, 2 + i).start()
+
+    def tree_last(k):
+        row_copy(k, partner, partner, 1).wait_recv()
+
+        @pl.when(~is_inner)
+        def _():
+            for t in (far_inner, far_outer):
+                row_copy(k, t, partner, 0).wait_recv()
+
+    def tree_drain(k):
+        @pl.when(is_inner)
+        def _():
+            for i in range(2):
+                far_copy(k, i).wait_send()
+                row_copy(k, far_outer if i else far_inner, partner, 2 + i).wait_send()
+
+        @pl.when(~is_inner)
+        def _():
+            pair_copy(k).wait_send()
+
+        partner_copy(k).wait_send()
+        row_copy(k, j, far_inner, 0).wait_send()
+        row_copy(k, j, partner, 1).wait_send()
+
     for k in range(CHUNKS):
-        begin(k)
+        tree_begin(k) if tree else begin(k)
+
+    rows_node = VOCAB // nodes
+    owner = lax.shift_right_logical(ids_ref[...], rows_node.bit_length() - 1).astype(F32)
+    shape = (slots, slots)
+    earlier = (column(owner, slots) == owner) & (iota(shape, 0) < iota(shape, 1))
+    rank = jnp.sum(jnp.where(earlier, 1.0, 0.0), axis=0, keepdims=True)
+    sent = column(owner * float(cap) + rank, slots)
+    shape = (slots, stacked)
+    sent = jnp.sum(
+        jnp.where(iota(shape, 0) == mod(iota(shape, 1), slots), sent, 0.0), axis=0, keepdims=True
+    )
+    shape = route.shape
+    sub, lane = iota(shape, 0), iota(shape, 1)
+    wanted = (div(sub, TILE) * cap + div(mod(sub, TILE), group)).astype(F32)
+    routed = jnp.where((wanted == sent) & (mod(sub, group) == div(lane, slots)), 1.0, 0.0).astype(F32)
+    route[...] = routed.astype(BF16)
+
+    shape = (nodes, nodes * TILE)
+    sub, lane = iota(shape, 0), iota(shape, 1)
+    place = jnp.zeros((1, nodes * TILE), F32)
+    for c in range(cap):
+        held = column(omap_ref[c : c + 1, :].astype(F32), nodes)
+        here = (sub == div(lane, TILE)) & (div(mod(lane, TILE), group) == c)
+        place = place + jnp.sum(jnp.where(here, held, 0.0), axis=0, keepdims=True)
+    shape = collect.shape
+    sub, lane = iota(shape, 0), iota(shape, 1)
+    taken = jnp.where(
+        (mod(sub, TILE).astype(F32) == place) & (div(sub, TILE) == mod(lane, group)), 1.0, 0.0
+    ).astype(F32)
+    collect[...] = taken.astype(BF16)
+
     route_t[...] = routed.T.astype(BF16)
     collect_t[...] = taken.T.astype(BF16)
-    stages = (near, far, forward, update, listed, first_hop, middle_hops, last_hop)
+    kept = column(touched_ref[...].astype(F32), touched_ref.shape[1]) >= 0.0
+
+    if tree:
+        stages = (merge, tree_forward, update, tree_listed, tree_pass, tree_last)
+    else:
+        stages = (near, far, forward, update, listed, first_hop, middle_hops, last_hop)
     for tick in range(CHUNKS + len(stages) - 1):
         for depth in reversed(range(len(stages))):
             if 0 <= tick - depth < CHUNKS:
@@ -379,6 +511,9 @@
     for k in range(CHUNKS):
         wait_nodes(k, fwd_src, fwd_ss)
         wait_nodes(k, rep_src, rep_ss)
+        if tree:
+            tree_drain(k)
+            continue
 
         def drain(s):
             @pl.when(last - s > j)
@@ -461,7 +596,7 @@
             dma((CHUNKS, locals_)),
         ],
         compiler_params=pltpu.CompilerParams(
-            collective_id=0, has_side_effects=True, vmem_limit_bytes=44 * 1024 * 1024
+            collective_id=0, has_side_effects=True, vmem_limit_bytes=56 * 1024 * 1024
         ),
     )(
         token_slot.reshape(1, tokens),

time: 53.1 us -> 46.1 us (0.87)
  local copies, waits for them, and re-layouts: 6.91 us -> 0.03 us
  Pallas kernels: 41.8 us -> 40.6 us
  matrix products: 1.64 us -> 2.83 us
    unnamed x16 -> x10, local copies, waits for them, and re-layouts: 6.91 us -> 0.03 us
    pallas_call x1, Pallas kernels: 41.8 us -> 40.6 us  [on_device(): pl.pallas_call(functools.partial(kernel, nodes, locals_, cap), out_shape=...]
    dot_general x1, matrix products: 1.64 us -> 2.83 us  [dot(): return jnp.dot(a, b, preferred_element_type=F32)]
where the time goes in v3:
time: 46.1 us; the launch traced here: 45.9 us
  Pallas kernels  40.6 us (88%)
  matrix products  2.83 us (6%)
  other arithmetic  1.81 us (4%)
  between operations  0.7 us (2%)
    pallas_call x1, Pallas kernels, on_device(): pl.pallas_call(functools.partial(kernel, nodes, locals_, cap), out_shape=...  40.6 us
    dot_general x1, matrix products, dot(): return jnp.dot(a, b, preferred_element_type=F32)  2.83 us
    select_n x1, other arithmetic, adam_rows(): jnp.where(kept, master_new, master)  1.14 us

profile of v3, /device:TPU:0, one launch (start us, length us, event | category | flops | bytes accessed | tf_op | source)
XLA Modules:
  0.0 45.9 jit_solution(8791336142067943079)
XLA Ops:
  0.6 0.0 copy-start.4
  0.6 0.7 %broadcast_compare_fusion = pred[16]{0:T(512)(128)(4,1)S(1)} fusion(s32[16]{0:T(128)} %param.11), kind=kLoop, calls=%fused_computation.9 | loop fusion | flops 16 | bytes 80 | tf_op jit(solution)/shard_map/ge | solution.py:612
  1.3 40.6 %shard_map.111 = (bf16[64,5376]{1,0:T(8,128)(2,1)}, f32[16,5376]{1,0:T(8,128)}) custom-call(s32[1,128]{1,0:T(1,128)} %bitcast.6, s32[1,16]{1,0:T(1,128)} %ids_ref.1, s32[1,16]{1,0:T(1,128)} %bitcast.8, s32[2,8]{1,0:T(2,128)} %bitcast.7, bf16[128,5376]{1,0:T(8,128)(2,1)} %grads_hbm.1, f32[16,5376]{1,0:T(8,128)} %moment_hbm.1, f32[16,5376]{1,0:T(8,128)} %second_hbm.1, ...), custom_call_target="tpu_custom_call" | custom-call | tf_op jit(solution)/shard_map/pallas_call | solution.py:557
  41.9 0.0 copy-start
  41.9 0.0 copy-start.1
  41.9 0.0 copy-start.2
  41.9 0.0 copy-start.3
  41.9 0.0 copy-done.4
  41.9 2.8 %convolution_convert_fusion = bf16[128,5376]{1,0:T(8,128)(2,1)} fusion(bf16[64,5376]{1,0:T(8,128)(2,1)} %get-tuple-element.6, s32[128]{0:T(128)S(1)} %copy-done.4), kind=kOutput, calls=%fused_computation | convolution fusion | flops 88776704 | bytes 2064896 | tf_op jit(solution)/shard_map/dot_general | solution.py:58
  44.8 0.0 copy-done
  44.8 0.0 copy-done.1
  44.8 0.0 copy-done.2
  44.8 0.0 copy-done.3
  44.8 1.1 %subtract_select_fusion = (f32[16,5376]{1,0:T(8,128)}, f32[16,5376]{1,0:T(8,128)}, f32[16,5376]{1,0:T(8,128)}) fusion(f32[16,5376]{1,0:T(8,128)S(1)} %copy-done.2, f32[16,5376]{1,0:T(8,128)S(1)} %copy-done.3, f32[16,5376]{1,0:T(8,128)S(1)} %copy-done, f32[16,5376]{1,0:T(8,128)S(1)} %copy-done.1, pred[16]{0:T(512)(128)(4,1)S(1)} %broadcast_compare_fusion), kind=kLoop, calls=%fused_computation.1 | loop fusion | flops 1290240 | bytes 2408464 | tf_op jit(solution)/shard_map/jit(_where)/select_n | solution.py:37
Async XLA Ops:
  0.6 41.3 %copy-start.4 = (s32[128]{0:T(128)S(1)}, s32[128]{0:T(128)}, u32[]{:S(2)}) copy-start(s32[128]{0:T(128)} %param.9) | copy-start | bytes 1540
  41.9 2.9 %copy-start = (f32[16,5376]{1,0:T(8,128)S(1)}, f32[16,5376]{1,0:T(8,128)}, u32[]{:S(2)}) copy-start(f32[16,5376]{1,0:T(8,128)} %moment_hbm.1) | copy-start | bytes 1032196
  41.9 2.9 %copy-start.1 = (f32[16,5376]{1,0:T(8,128)S(1)}, f32[16,5376]{1,0:T(8,128)}, u32[]{:S(2)}) copy-start(f32[16,5376]{1,0:T(8,128)} %second_hbm.1) | copy-start | bytes 1032196
  41.9 2.9 %copy-start.2 = (f32[16,5376]{1,0:T(8,128)S(1)}, f32[16,5376]{1,0:T(8,128)}, u32[]{:S(2)}) copy-start(f32[16,5376]{1,0:T(8,128)} %master_hbm.1) | copy-start | bytes 1032196
  41.9 2.9 %copy-start.3 = (f32[16,5376]{1,0:T(8,128)S(1)}, f32[16,5376]{1,0:T(8,128)}, u32[]{:S(2)}) copy-start(f32[16,5376]{1,0:T(8,128)} %get-tuple-element.7) | copy-start | bytes 1032196

commit v4 on v3

--- a/solution.py
+++ b/solution.py
@@ -16,7 +16,7 @@
 EPSILON = 1e-08
 
 MESH = pl.DeviceIdType.MESH
-CHUNKS = 3
+CHUNKS = 6
 BLOCKS = 7
 TILE = 16
 F32 = jnp.float32

time: 46.1 us -> 54 us (1.17)
  Pallas kernels: 40.6 us -> 48.4 us
    pallas_call x1, Pallas kernels: 40.6 us -> 48.4 us  [on_device(): pl.pallas_call(functools.partial(kernel, nodes, locals_, cap), out_shape=...]
where the time goes in v4:
time: 54 us; the launch traced here: 53.8 us
  Pallas kernels  48.4 us (90%)
  matrix products  2.83 us (5%)
  other arithmetic  1.81 us (3%)
  between operations  0.7 us (1%)
    pallas_call x1, Pallas kernels, on_device(): pl.pallas_call(functools.partial(kernel, nodes, locals_, cap), out_shape=...  48.4 us
    dot_general x1, matrix products, dot(): return jnp.dot(a, b, preferred_element_type=F32)  2.83 us
    select_n x1, other arithmetic, adam_rows(): jnp.where(kept, master_new, master)  1.14 us

profile of v4, /device:TPU:0, one launch (start us, length us, event | category | flops | bytes accessed | tf_op | source)
XLA Modules:
  0.0 53.8 jit_solution(11586599252321374101)
XLA Ops:
  0.6 0.0 copy-start.4
  0.6 0.7 %broadcast_compare_fusion = pred[16]{0:T(512)(128)(4,1)S(1)} fusion(s32[16]{0:T(128)} %param.11), kind=kLoop, calls=%fused_computation.9 | loop fusion | flops 16 | bytes 80 | tf_op jit(solution)/shard_map/ge | solution.py:612
  1.3 48.4 %shard_map.111 = (bf16[64,5376]{1,0:T(8,128)(2,1)}, f32[16,5376]{1,0:T(8,128)}) custom-call(s32[1,128]{1,0:T(1,128)} %bitcast.6, s32[1,16]{1,0:T(1,128)} %ids_ref.1, s32[1,16]{1,0:T(1,128)} %bitcast.8, s32[2,8]{1,0:T(2,128)} %bitcast.7, bf16[128,5376]{1,0:T(8,128)(2,1)} %grads_hbm.1, f32[16,5376]{1,0:T(8,128)} %moment_hbm.1, f32[16,5376]{1,0:T(8,128)} %second_hbm.1, ...), custom_call_target="tpu_custom_call" | custom-call | tf_op jit(solution)/shard_map/pallas_call | solution.py:557
  49.8 0.0 copy-start
  49.8 0.0 copy-start.1
  49.8 0.0 copy-start.2
  49.8 0.0 copy-start.3
  49.8 0.0 copy-done.4
  49.8 2.8 %convolution_convert_fusion = bf16[128,5376]{1,0:T(8,128)(2,1)} fusion(bf16[64,5376]{1,0:T(8,128)(2,1)} %get-tuple-element.6, s32[128]{0:T(128)S(1)} %copy-done.4), kind=kOutput, calls=%fused_computation | convolution fusion | flops 88776704 | bytes 2064896 | tf_op jit(solution)/shard_map/dot_general | solution.py:58
  52.7 0.0 copy-done
  52.7 0.0 copy-done.1
  52.7 0.0 copy-done.2
  52.7 0.0 copy-done.3
  52.7 1.1 %subtract_select_fusion = (f32[16,5376]{1,0:T(8,128)}, f32[16,5376]{1,0:T(8,128)}, f32[16,5376]{1,0:T(8,128)}) fusion(f32[16,5376]{1,0:T(8,128)S(1)} %copy-done.2, f32[16,5376]{1,0:T(8,128)S(1)} %copy-done.3, f32[16,5376]{1,0:T(8,128)S(1)} %copy-done, f32[16,5376]{1,0:T(8,128)S(1)} %copy-done.1, pred[16]{0:T(512)(128)(4,1)S(1)} %broadcast_compare_fusion), kind=kLoop, calls=%fused_computation.1 | loop fusion | flops 1290240 | bytes 2408464 | tf_op jit(solution)/shard_map/jit(_where)/select_n | solution.py:37
Async XLA Ops:
  0.6 49.2 %copy-start.4 = (s32[128]{0:T(128)S(1)}, s32[128]{0:T(128)}, u32[]{:S(2)}) copy-start(s32[128]{0:T(128)} %param.9) | copy-start | bytes 1540
  49.8 2.9 %copy-start = (f32[16,5376]{1,0:T(8,128)S(1)}, f32[16,5376]{1,0:T(8,128)}, u32[]{:S(2)}) copy-start(f32[16,5376]{1,0:T(8,128)} %moment_hbm.1) | copy-start | bytes 1032196
  49.8 2.9 %copy-start.1 = (f32[16,5376]{1,0:T(8,128)S(1)}, f32[16,5376]{1,0:T(8,128)}, u32[]{:S(2)}) copy-start(f32[16,5376]{1,0:T(8,128)} %second_hbm.1) | copy-start | bytes 1032196
  49.8 2.9 %copy-start.2 = (f32[16,5376]{1,0:T(8,128)S(1)}, f32[16,5376]{1,0:T(8,128)}, u32[]{:S(2)}) copy-start(f32[16,5376]{1,0:T(8,128)} %master_hbm.1) | copy-start | bytes 1032196
  49.8 2.9 %copy-start.3 = (f32[16,5376]{1,0:T(8,128)S(1)}, f32[16,5376]{1,0:T(8,128)}, u32[]{:S(2)}) copy-start(f32[16,5376]{1,0:T(8,128)} %get-tuple-element.7) | copy-start | bytes 1032196

commit v5 on v3

--- a/solution.py
+++ b/solution.py
@@ -52,6 +52,15 @@
 
 def mod(x, m):
     return x & (m - 1) if m & (m - 1) == 0 else x % m
+
+
+def iota(shape, dim):
+    return lax.broadcasted_iota(jnp.int32, shape, dim)
+
+
+def column(row, size):
+    diagonal = iota((size, size), 0) == iota((size, size), 1)
+    return jnp.sum(jnp.where(diagonal, row, 0.0), axis=1, keepdims=True)
 
 
 def dot(a, b):
@@ -158,13 +167,6 @@
         line_peers = jnp.minimum(j, 1) + jnp.minimum(last - j, 1)
     repeat(nodes - 1, greet)
 
-    def iota(shape, dim):
-        return lax.broadcasted_iota(jnp.int32, shape, dim)
-
-    def column(row, size):
-        diagonal = iota((size, size), 0) == iota((size, size), 1)
-        return jnp.sum(jnp.where(diagonal, row, 0.0), axis=1, keepdims=True)
-
     shape = select.shape
     select[...] = jnp.where(iota(shape, 0) == slot_ref[...], 1.0, 0.0).astype(BF16)
 
@@ -504,7 +506,7 @@
     else:
         stages = (near, far, forward, update, listed, first_hop, middle_hops, last_hop)
     for tick in range(CHUNKS + len(stages) - 1):
-        for depth in reversed(range(len(stages))):
+        for depth in range(len(stages)):
             if 0 <= tick - depth < CHUNKS:
                 stages[depth](tick - depth)
 
@@ -536,6 +538,65 @@
                 ag_copy(k, t, False).wait_send()
 
         repeat(locals_, drain_gather)
+
+
+def write_kernel(
+    slot_ref,
+    touched_ref,
+    rows,
+    gradient,
+    moment,
+    second,
+    master,
+    tok_out,
+    moment_out,
+    second_out,
+    master_out,
+    select_t,
+):
+    @pl.when(pl.program_id(0) == 0)
+    def _():
+        shape = (rows.shape[0], tok_out.shape[0])
+        chosen = jnp.where(iota(shape, 0) == slot_ref[...], 1.0, 0.0).astype(F32)
+        select_t[...] = chosen.T.astype(BF16)
+
+    kept = column(touched_ref[...].astype(F32), touched_ref.shape[1]) >= 0.0
+    moment_out[...], second_out[...], master_out[...] = adam_rows(
+        gradient[...], moment[...], second[...], master[...], kept
+    )
+    tok_out[...] = dot(select_t[...], rows[...]).astype(BF16)
+
+
+def write_out(token_slot, touched_ids, rows, gradient, moment, second, master):
+    tokens, touch = token_slot.shape[0], touched_ids.shape[0]
+    list_len, width = rows.shape
+    steps = 3
+    block = width // steps
+
+    def small(count):
+        return pl.BlockSpec((1, count), lambda i: (0, 0))
+
+    def tall(count):
+        return pl.BlockSpec((count, block), lambda i: (0, i))
+
+    return pl.pallas_call(
+        write_kernel,
+        grid=(steps,),
+        out_shape=(jax.ShapeDtypeStruct((tokens, width), BF16),)
+        + (jax.ShapeDtypeStruct((touch, width), F32),) * 3,
+        in_specs=[small(tokens), small(touch), tall(list_len)] + [tall(touch)] * 4,
+        out_specs=[tall(tokens)] + [tall(touch)] * 3,
+        scratch_shapes=[pltpu.VMEM((tokens, list_len), BF16)],
+        compiler_params=pltpu.CompilerParams(vmem_limit_bytes=56 * 1024 * 1024),
+    )(
+        token_slot.reshape(1, tokens),
+        touched_ids.reshape(1, touch),
+        rows,
+        gradient,
+        moment,
+        second,
+        master,
+    )
 
 
 def on_device(nodes, locals_, grads, token_slot, node_ids, touched_ids, owner_map, moment, second, master):
@@ -608,12 +669,7 @@
         second,
         master,
     )
-    moment_out, second_out, master_out = adam_rows(
-        gradient, moment, second, master, touched_ids[:, None] >= 0
-    )
-    wanted = lax.iota(jnp.int32, list_len)
-    selector = (token_slot[:, None] == wanted[None, :]).astype(BF16)
-    return dot(selector, rows).astype(BF16), moment_out, second_out, master_out
+    return write_out(token_slot, touched_ids, rows, gradient, moment, second, master)
 
 
 def solution(mesh):

time: 46.1 us -> 44.4 us (0.963)
  Pallas kernels: 40.6 us -> 43.6 us
  matrix products: 2.83 us -> 0 us
  other arithmetic: 1.81 us -> 0 us
    pallas_call x0 -> x1, Pallas kernels: none -> 4.4 us  [write_out(): pl.pallas_call(write_kernel, grid=(steps,), out_shape=(jax.ShapeDtypeStru...]
    dot_general x1 -> x0, matrix products: 2.83 us -> none  [dot(): return jnp.dot(a, b, preferred_element_type=F32)]
    pallas_call x1, Pallas kernels: 40.6 us -> 39.2 us  [on_device(): pl.pallas_call(functools.partial(kernel, nodes, locals_, cap), out_shape=...]
    select_n x1 -> x0, other arithmetic: 1.14 us -> none  [adam_rows(): jnp.where(kept, master_new, master)]
    ge x1 -> x0, other arithmetic: 0.67 us -> none  [on_device(): touched_ids[:, None] >= 0]
where the time goes in v5:
time: 44.4 us; the launch traced here: 44.2 us
  Pallas kernels  43.6 us (98%)
  between operations  0.64 us (1%)
    pallas_call x1, Pallas kernels, on_device(): pl.pallas_call(functools.partial(kernel, nodes, locals_, cap), out_shape=...  39.2 us
    pallas_call x1, Pallas kernels, write_out(): pl.pallas_call(write_kernel, grid=(steps,), out_shape=(jax.ShapeDtypeStru...  4.4 us

profile of v5, /device:TPU:0, one launch (start us, length us, event | category | flops | bytes accessed | tf_op | source)
XLA Modules:
  0.0 44.2 jit_solution(8445038349047768150)
XLA Ops:
  0.6 39.2 %shard_map.111 = (bf16[64,5376]{1,0:T(8,128)(2,1)}, f32[16,5376]{1,0:T(8,128)}) custom-call(s32[1,128]{1,0:T(1,128)} %bitcast.5, s32[1,16]{1,0:T(1,128)} %ids_ref.1, s32[1,16]{1,0:T(1,128)} %bitcast.7, s32[2,8]{1,0:T(2,128)} %bitcast.9, bf16[128,5376]{1,0:T(8,128)(2,1)} %grads_hbm.1, f32[16,5376]{1,0:T(8,128)} %moment.1, f32[16,5376]{1,0:T(8,128)} %second.1, ...), custom_call_target="tpu_custom_call" | custom-call | tf_op jit(solution)/shard_map/pallas_call | solution.py:618
  39.8 4.4 %shard_map.112 = (bf16[128,5376]{1,0:T(8,128)(2,1)}, f32[16,5376]{1,0:T(8,128)}, f32[16,5376]{1,0:T(8,128)}, f32[16,5376]{1,0:T(8,128)}) custom-call(s32[1,128]{1,0:T(1,128)} %bitcast.6, s32[1,16]{1,0:T(1,128)} %bitcast.8, bf16[64,5376]{1,0:T(8,128)(2,1)} %get-tuple-element.6.rows, f32[16,5376]{1,0:T(8,128)} %get-tuple-element.7.gradient, ...), custom_call_target="tpu_custom_call" | custom-call | tf_op jit(solution)/shard_map/pallas_call | solution.py:582

commit v6 on v5

--- a/solution.py
+++ b/solution.py
@@ -16,8 +16,9 @@
 EPSILON = 1e-08
 
 MESH = pl.DeviceIdType.MESH
-CHUNKS = 3
+CHUNKS = 2
 BLOCKS = 7
+PIECES = 3
 TILE = 16
 F32 = jnp.float32
 BF16 = jnp.bfloat16
@@ -543,50 +544,84 @@
 def write_kernel(
     slot_ref,
     touched_ref,
+    rows_hbm,
+    gradient_hbm,
+    moment_hbm,
+    second_hbm,
+    master_hbm,
+    tok_hbm,
+    moment_out_hbm,
+    second_out_hbm,
+    master_out_hbm,
     rows,
-    gradient,
-    moment,
-    second,
-    master,
-    tok_out,
-    moment_out,
-    second_out,
-    master_out,
-    select_t,
+    states,
+    tok,
+    news,
+    rows_sem,
+    state_sem,
+    tok_sem,
+    new_sem,
 ):
-    @pl.when(pl.program_id(0) == 0)
-    def _():
-        shape = (rows.shape[0], tok_out.shape[0])
-        chosen = jnp.where(iota(shape, 0) == slot_ref[...], 1.0, 0.0).astype(F32)
-        select_t[...] = chosen.T.astype(BF16)
-
+    width = rows.shape[1]
+    block = width // PIECES
+    pieces = [pl.ds(p * block, block) for p in range(PIECES)]
+    row_loads = [
+        pltpu.make_async_copy(rows_hbm.at[:, c], rows.at[:, c], rows_sem.at[p])
+        for p, c in enumerate(pieces)
+    ]
+    state_loads = [
+        pltpu.make_async_copy(ref, states.at[i], state_sem.at[i])
+        for i, ref in enumerate((gradient_hbm, moment_hbm, second_hbm, master_hbm))
+    ]
+    for copy in row_loads + state_loads:
+        copy.start()
+    shape = (rows.shape[0], tok.shape[0])
+    chosen = jnp.where(iota(shape, 0) == slot_ref[...], 1.0, 0.0).astype(F32)
+    select_t = chosen.T.astype(BF16)
     kept = column(touched_ref[...].astype(F32), touched_ref.shape[1]) >= 0.0
-    moment_out[...], second_out[...], master_out[...] = adam_rows(
-        gradient[...], moment[...], second[...], master[...], kept
-    )
-    tok_out[...] = dot(select_t[...], rows[...]).astype(BF16)
+    stores = []
+    for p, c in enumerate(pieces):
+        row_loads[p].wait()
+        tok[:, c] = dot(select_t, rows[:, c]).astype(BF16)
+        stores.append(pltpu.make_async_copy(tok.at[:, c], tok_hbm.at[:, c], tok_sem.at[p]))
+        stores[-1].start()
+    for copy in state_loads:
+        copy.wait()
+    for p, c in enumerate(pieces):
+        new = adam_rows(states[0, :, c], states[1, :, c], states[2, :, c], states[3, :, c], kept)
+        outs = (moment_out_hbm, second_out_hbm, master_out_hbm)
+        for i, (value, out) in enumerate(zip(new, outs)):
+            news[i, :, c] = value
+            stores.append(
+                pltpu.make_async_copy(news.at[i, :, c], out.at[:, c], new_sem.at[i, p])
+            )
+            stores[-1].start()
+    for copy in stores:
+        copy.wait()
 
 
 def write_out(token_slot, touched_ids, rows, gradient, moment, second, master):
     tokens, touch = token_slot.shape[0], touched_ids.shape[0]
     list_len, width = rows.shape
-    steps = 3
-    block = width // steps
-
-    def small(count):
-        return pl.BlockSpec((1, count), lambda i: (0, 0))
-
-    def tall(count):
-        return pl.BlockSpec((count, block), lambda i: (0, i))
-
+    vmem = pl.BlockSpec(memory_space=pltpu.VMEM)
+    hbm = pl.BlockSpec(memory_space=pltpu.HBM)
+    dma = pltpu.SemaphoreType.DMA
     return pl.pallas_call(
         write_kernel,
-        grid=(steps,),
         out_shape=(jax.ShapeDtypeStruct((tokens, width), BF16),)
         + (jax.ShapeDtypeStruct((touch, width), F32),) * 3,
-        in_specs=[small(tokens), small(touch), tall(list_len)] + [tall(touch)] * 4,
-        out_specs=[tall(tokens)] + [tall(touch)] * 3,
-        scratch_shapes=[pltpu.VMEM((tokens, list_len), BF16)],
+        in_specs=[vmem] * 2 + [hbm] * 5,
+        out_specs=[hbm] * 4,
+        scratch_shapes=[
+            pltpu.VMEM((list_len, width), BF16),
+            pltpu.VMEM((4, touch, width), F32),
+            pltpu.VMEM((tokens, width), BF16),
+            pltpu.VMEM((3, touch, width), F32),
+            dma((PIECES,)),
+            dma((4,)),
+            dma((PIECES,)),
+            dma((3, PIECES)),
+        ],
         compiler_params=pltpu.CompilerParams(vmem_limit_bytes=56 * 1024 * 1024),
     )(
         token_slot.reshape(1, tokens),

time: 44.4 us -> 46.8 us (1.054)
  Pallas kernels: 43.6 us -> 46 us
    pallas_call x1, Pallas kernels: 39.2 us -> 42.2 us  [on_device(): pl.pallas_call(functools.partial(kernel, nodes, locals_, cap), out_shape=...]
    pallas_call x1, Pallas kernels: 4.4 us -> 3.79 us  [write_out(): pl.pallas_call(write_kernel, out_shape=(jax.ShapeDtypeStruct((tokens, wid...]
where the time goes in v6:
time: 46.8 us; the launch traced here: 46.6 us
  Pallas kernels  46 us (98%)
  between operations  0.64 us (1%)
    pallas_call x1, Pallas kernels, on_device(): pl.pallas_call(functools.partial(kernel, nodes, locals_, cap), out_shape=...  42.2 us
    pallas_call x1, Pallas kernels, write_out(): pl.pallas_call(write_kernel, out_shape=(jax.ShapeDtypeStruct((tokens, wid...  3.79 us

profile of v6, /device:TPU:0, one launch (start us, length us, event | category | flops | bytes accessed | tf_op | source)
XLA Modules:
  0.0 46.6 jit_solution(4992082629544377190)
XLA Ops:
  0.6 42.2 %shard_map.111 = (bf16[64,5376]{1,0:T(8,128)(2,1)}, f32[16,5376]{1,0:T(8,128)}) custom-call(s32[1,128]{1,0:T(1,128)} %bitcast.5, s32[1,16]{1,0:T(1,128)} %ids_ref.1, s32[1,16]{1,0:T(1,128)} %bitcast.7, s32[2,8]{1,0:T(2,128)} %bitcast.9, bf16[128,5376]{1,0:T(8,128)(2,1)} %grads_hbm.1, f32[16,5376]{1,0:T(8,128)} %moment_hbm.3, f32[16,5376]{1,0:T(8,128)} %second_hbm.3, ...), custom_call_target="tpu_custom_call" | custom-call | tf_op jit(solution)/shard_map/pallas_call | solution.py:653
  42.8 3.8 %shard_map.112 = (bf16[128,5376]{1,0:T(8,128)(2,1)}, f32[16,5376]{1,0:T(8,128)}, f32[16,5376]{1,0:T(8,128)}, f32[16,5376]{1,0:T(8,128)}) custom-call(s32[1,128]{1,0:T(1,128)} %bitcast.6, s32[1,16]{1,0:T(1,128)} %bitcast.8, bf16[64,5376]{1,0:T(8,128)(2,1)} %get-tuple-element.6.rows_hbm, f32[16,5376]{1,0:T(8,128)} %get-tuple-element.7.gradient_hbm, ...), custom_call_target="tpu_custom_call" | custom-call | tf_op jit(solution)/shard_map/pallas_call | solution.py:609

commit v7 on v6

--- a/solution.py
+++ b/solution.py
@@ -16,7 +16,8 @@
 EPSILON = 1e-08
 
 MESH = pl.DeviceIdType.MESH
-CHUNKS = 2
+SHARES = (1, 2, 2, 1)
+CHUNKS = len(SHARES)
 BLOCKS = 7
 PIECES = 3
 TILE = 16
@@ -66,6 +67,12 @@
 
 def dot(a, b):
     return jnp.dot(a, b, preferred_element_type=F32)
+
+
+def chunk_widths(width):
+    unit = width // sum(SHARES)
+    cws = [unit * share for share in SHARES]
+    return cws, [sum(cws[:k]) for k in range(CHUNKS)]
 
 
 def kernel(
@@ -119,15 +126,15 @@
     last = locals_ - 1
     half = locals_ // 2
     width = grads.shape[1]
-    cw = width // CHUNKS
-    bw = cw // BLOCKS
-    slots = part.shape[2]
+    cws, starts = chunk_widths(width)
+    bws = [cw // BLOCKS for cw in cws]
+    slots = part[0].shape[1]
     group = TILE // cap
     stacked = BLOCKS * slots
 
     loads = []
     for k in range(CHUNKS):
-        cols = pl.ds(k * cw, cw)
+        cols = pl.ds(starts[k], cws[k])
         loads.append(
             pltpu.make_async_copy(grads_hbm.at[:, cols], grads.at[:, cols], load_sem.at[k])
         )
@@ -175,8 +182,8 @@
 
     def up_copy(k, s):
         return pltpu.make_async_remote_copy(
-            up_src.at[k, s],
-            up_dst.at[k, s],
+            up_src[k].at[s],
+            up_dst[k].at[s],
             up_ss.at[k, s],
             up_rs.at[k, s],
             device_id=(n, jnp.minimum(j + 1, last)),
@@ -185,8 +192,8 @@
 
     def dn_copy(k, s):
         return pltpu.make_async_remote_copy(
-            dn_src.at[k, s],
-            dn_dst.at[k, s],
+            dn_src[k].at[s],
+            dn_dst[k].at[s],
             dn_ss.at[k, s],
             dn_rs.at[k, s],
             device_id=(n, jnp.maximum(j - 1, 0)),
@@ -194,7 +201,7 @@
         )
 
     def ag_copy(k, t, up):
-        rows = gath.at[pl.ds(pl.multiple_of(t * slots, slots), slots), pl.ds(k * cw, cw)]
+        rows = gath.at[pl.ds(pl.multiple_of(t * slots, slots), slots), pl.ds(starts[k], cws[k])]
         return pltpu.make_async_remote_copy(
             rows,
             rows,
@@ -208,8 +215,8 @@
         def send(p):
             peer = lax.rem(n + p + 1, nodes)
             pltpu.make_async_remote_copy(
-                src.at[k, peer],
-                dst.at[k, n],
+                src[k].at[peer],
+                dst[k].at[n],
                 ss.at[k],
                 rs.at[k],
                 device_id=(peer, j),
@@ -217,16 +224,16 @@
             ).start()
 
         repeat(nodes - 1, send)
-        dst[k, n] = src[k, n]
+        dst[k][n] = src[k][n]
 
     def wait_nodes(k, buf, sem):
-        whole = buf.at[k, pl.ds(0, nodes - 1)]
+        whole = buf[k].at[pl.ds(0, nodes - 1)]
         pltpu.make_async_copy(whole, whole, sem.at[k]).wait()
 
     def sums(k):
         loads[k].wait()
-        total = dot(select[...], grads[:, k * cw : (k + 1) * cw])
-        part[k] = total.reshape(locals_, slots, cw)
+        total = dot(select[...], grads[:, starts[k] : starts[k] + cws[k]])
+        part[k][...] = total.reshape(locals_, slots, cws[k])
 
     def begin(k):
         sums(k)
@@ -234,7 +241,7 @@
         @pl.when(j == 0)
         def _():
             def step(s):
-                up_src[k, s] = part[k, last - s].astype(BF16)
+                up_src[k][s] = part[k][last - s].astype(BF16)
                 up_copy(k, s).start()
 
             repeat(last, step)
@@ -242,7 +249,7 @@
         @pl.when(j == last)
         def _():
             def step(s):
-                dn_src[k, s] = part[k, s].astype(BF16)
+                dn_src[k][s] = part[k][s].astype(BF16)
                 dn_copy(k, s).start()
 
             repeat(last, step)
@@ -252,7 +259,7 @@
             @pl.when(last - s > j)
             def _():
                 up_copy(k, s).wait_recv()
-                up_src[k, s] = (up_dst[k, s].astype(F32) + part[k, last - s]).astype(BF16)
+                up_src[k][s] = (up_dst[k][s].astype(F32) + part[k][last - s]).astype(BF16)
                 up_copy(k, s).start()
 
         repeat(last, step)
@@ -262,7 +269,7 @@
             @pl.when(s < j)
             def _():
                 dn_copy(k, s).wait_recv()
-                dn_src[k, s] = (dn_dst[k, s].astype(F32) + part[k, s]).astype(BF16)
+                dn_src[k][s] = (dn_dst[k][s].astype(F32) + part[k][s]).astype(BF16)
                 dn_copy(k, s).start()
 
         repeat(last, step)
@@ -279,19 +286,19 @@
         @pl.when(j > 0)
         def _():
             up_copy(k, last - j).wait_recv()
-            part[k, j] = part[k, j] + up_dst[k, last - j].astype(F32)
+            part[k][j] = part[k][j] + up_dst[k][last - j].astype(F32)
 
         @pl.when(j < last)
         def _():
             dn_copy(k, j).wait_recv()
-            part[k, j] = part[k, j] + dn_dst[k, j].astype(F32)
-
-        send_out(k, part[k, j])
+            part[k][j] = part[k][j] + dn_dst[k][j].astype(F32)
+
+        send_out(k, part[k][j])
 
     def send_out(k, total):
         own = total.astype(BF16)
-        tall = jnp.concatenate([own[:, b * bw : (b + 1) * bw] for b in range(BLOCKS)], axis=0)
-        fwd_src[k] = dot(route[...], tall).astype(BF16).reshape(nodes, TILE, bw)
+        tall = jnp.concatenate([own[:, b * bws[k] : (b + 1) * bws[k]] for b in range(BLOCKS)], axis=0)
+        fwd_src[k][...] = dot(route[...], tall).astype(BF16).reshape(nodes, TILE, bws[k])
         send_nodes(k, fwd_src, fwd_dst, fwd_ss, fwd_rs)
 
     def update(k):
@@ -299,10 +306,10 @@
             for copy in adam_loads:
                 copy.wait()
         wait_nodes(k, fwd_dst, fwd_rs)
-        gradient = dot(collect[...], fwd_dst[k].reshape(nodes * TILE, bw))
+        gradient = dot(collect[...], fwd_dst[k][...].reshape(nodes * TILE, bws[k]))
         fresh = []
         for b in range(BLOCKS):
-            cols = slice(k * cw + b * bw, k * cw + (b + 1) * bw)
+            cols = slice(starts[k] + b * bws[k], starts[k] + (b + 1) * bws[k])
             new = adam_rows(
                 gradient[b * TILE : (b + 1) * TILE],
                 moment[:, cols],
@@ -313,15 +320,15 @@
             gradient_out[:, cols] = gradient[b * TILE : (b + 1) * TILE]
             fresh.append(new[2].astype(BF16))
         tall = jnp.concatenate(fresh, axis=0)
-        rep_src[k] = dot(collect_t[...], tall).astype(BF16).reshape(nodes, TILE, bw)
+        rep_src[k][...] = dot(collect_t[...], tall).astype(BF16).reshape(nodes, TILE, bws[k])
         send_nodes(k, rep_src, rep_dst, rep_ss, rep_rs)
 
     def fill(k):
         wait_nodes(k, rep_dst, rep_rs)
-        rows = dot(route_t[...], rep_dst[k].reshape(nodes * TILE, bw)).astype(BF16)
+        rows = dot(route_t[...], rep_dst[k][...].reshape(nodes * TILE, bws[k])).astype(BF16)
         own = pl.ds(pl.multiple_of(j * slots, slots), slots)
         for b in range(BLOCKS):
-            cols = slice(k * cw + b * bw, k * cw + (b + 1) * bw)
+            cols = slice(starts[k] + b * bws[k], starts[k] + (b + 1) * bws[k])
             gath[own, cols] = rows[b * slots : (b + 1) * slots]
 
     def listed(k):
@@ -366,8 +373,8 @@
     def pair_copy(k):
         rows = pl.ds(0, 2)
         return pltpu.make_async_remote_copy(
-            up_src.at[k, rows],
-            up_dst.at[k, rows],
+            up_src[k].at[rows],
+            up_dst[k].at[rows],
             up_ss.at[k, 0],
             up_rs.at[k, 0],
             device_id=(n, partner),
@@ -376,8 +383,8 @@
 
     def partner_copy(k):
         return pltpu.make_async_remote_copy(
-            up_src.at[k, 2],
-            up_dst.at[k, 2],
+            up_src[k].at[2],
+            up_dst[k].at[2],
             up_ss.at[k, 2],
             up_rs.at[k, 1],
             device_id=(n, partner),
@@ -386,8 +393,8 @@
 
     def far_copy(k, i):
         return pltpu.make_async_remote_copy(
-            up_src.at[k, i],
-            dn_dst.at[k, 0],
+            up_src[k].at[i],
+            dn_dst[k].at[0],
             up_ss.at[k, i],
             up_rs.at[k, 2],
             device_id=(n, far_outer if i else far_inner),
@@ -395,7 +402,7 @@
         )
 
     def row_copy(k, t, peer, i):
-        rows = gath.at[pl.ds(pl.multiple_of(t * slots, slots), slots), pl.ds(k * cw, cw)]
+        rows = gath.at[pl.ds(pl.multiple_of(t * slots, slots), slots), pl.ds(starts[k], cws[k])]
         return pltpu.make_async_remote_copy(
             rows,
             rows,
@@ -410,11 +417,11 @@
 
         @pl.when(~is_inner)
         def _():
-            up_src[k, 0] = part[k, far_inner].astype(BF16)
-            up_src[k, 1] = part[k, far_outer].astype(BF16)
+            up_src[k][0] = part[k][far_inner].astype(BF16)
+            up_src[k][1] = part[k][far_outer].astype(BF16)
             pair_copy(k).start()
 
-        up_src[k, 2] = part[k, partner].astype(BF16)
+        up_src[k][2] = part[k][partner].astype(BF16)
         partner_copy(k).start()
 
     def merge(k):
@@ -422,13 +429,13 @@
         def _():
             pair_copy(k).wait_recv()
             for i, t in enumerate((far_inner, far_outer)):
-                up_src[k, i] = (up_dst[k, i].astype(F32) + part[k, t]).astype(BF16)
+                up_src[k][i] = (up_dst[k][i].astype(F32) + part[k][t]).astype(BF16)
                 far_copy(k, i).start()
 
     def tree_forward(k):
         partner_copy(k).wait_recv()
         far_copy(k, 0).wait_recv()
-        send_out(k, part[k, j] + up_dst[k, 2].astype(F32) + dn_dst[k, 0].astype(F32))
+        send_out(k, part[k][j] + up_dst[k][2].astype(F32) + dn_dst[k][0].astype(F32))
 
     def tree_listed(k):
         fill(k)
@@ -640,15 +647,14 @@
     touch = touched_ids.shape[0]
     cap = owner_map.shape[2]
     group = TILE // cap
-    cw = width // CHUNKS
-    bw = cw // BLOCKS
+    cws, _ = chunk_widths(width)
     last = locals_ - 1
     vmem = pl.BlockSpec(memory_space=pltpu.VMEM)
     hbm = pl.BlockSpec(memory_space=pltpu.HBM)
     dma = pltpu.SemaphoreType.DMA
     list_len = locals_ * slots
-    line = pltpu.VMEM((CHUNKS, last, slots, cw), BF16)
-    plane = pltpu.VMEM((CHUNKS, nodes, TILE, bw), BF16)
+    line = tuple(pltpu.VMEM((last, slots, cw), BF16) for cw in cws)
+    plane = tuple(pltpu.VMEM((nodes, TILE, cw // BLOCKS), BF16) for cw in cws)
     stacked = BLOCKS * slots
     rows, gradient = pl.pallas_call(
         functools.partial(kernel, nodes, locals_, cap),
@@ -668,7 +674,7 @@
             pltpu.VMEM((BLOCKS * touch, nodes * TILE), BF16),
             pltpu.VMEM((nodes * TILE, BLOCKS * touch), BF16),
             pltpu.VMEM((list_len, tokens), BF16),
-            pltpu.VMEM((CHUNKS, locals_, slots, cw), F32),
+            tuple(pltpu.VMEM((locals_, slots, cw), F32) for cw in cws),
             line,
             line,
             line,

time: 46.8 us -> 44.1 us (0.942)
  Pallas kernels: 46 us -> 43.3 us
    pallas_call x1, Pallas kernels: 42.2 us -> 39.5 us  [on_device(): pl.pallas_call(functools.partial(kernel, nodes, locals_, cap), out_shape=...]
where the time goes in v7:
time: 44.1 us; the launch traced here: 43.9 us
  Pallas kernels  43.3 us (98%)
  between operations  0.64 us (1%)
    pallas_call x1, Pallas kernels, on_device(): pl.pallas_call(functools.partial(kernel, nodes, locals_, cap), out_shape=...  39.5 us
    pallas_call x1, Pallas kernels, write_out(): pl.pallas_call(write_kernel, out_shape=(jax.ShapeDtypeStruct((tokens, wid...  3.79 us

profile of v7, /device:TPU:0, one launch (start us, length us, event | category | flops | bytes accessed | tf_op | source)
XLA Modules:
  0.0 43.9 jit_solution(12122623414672353162)
XLA Ops:
  0.6 39.5 %shard_map.111 = (bf16[64,5376]{1,0:T(8,128)(2,1)}, f32[16,5376]{1,0:T(8,128)}) custom-call(s32[1,128]{1,0:T(1,128)} %bitcast.5, s32[1,16]{1,0:T(1,128)} %ids_ref.1, s32[1,16]{1,0:T(1,128)} %bitcast.7, s32[2,8]{1,0:T(2,128)} %bitcast.9, bf16[128,5376]{1,0:T(8,128)(2,1)} %grads_hbm.1, f32[16,5376]{1,0:T(8,128)} %moment_hbm.3, f32[16,5376]{1,0:T(8,128)} %second_hbm.3, ...), custom_call_target="tpu_custom_call" | custom-call | tf_op jit(solution)/shard_map/pallas_call | solution.py:659
  40.1 3.8 %shard_map.112 = (bf16[128,5376]{1,0:T(8,128)(2,1)}, f32[16,5376]{1,0:T(8,128)}, f32[16,5376]{1,0:T(8,128)}, f32[16,5376]{1,0:T(8,128)}) custom-call(s32[1,128]{1,0:T(1,128)} %bitcast.6, s32[1,16]{1,0:T(1,128)} %bitcast.8, bf16[64,5376]{1,0:T(8,128)(2,1)} %get-tuple-element.6.rows_hbm, f32[16,5376]{1,0:T(8,128)} %get-tuple-element.7.gradient_hbm, ...), custom_call_target="tpu_custom_call" | custom-call | tf_op jit(solution)/shard_map/pallas_call | solution.py:616

commit v8 on v7

--- a/solution.py
+++ b/solution.py
@@ -16,7 +16,7 @@
 EPSILON = 1e-08
 
 MESH = pl.DeviceIdType.MESH
-SHARES = (1, 2, 2, 1)
+SHARES = (2, 2, 2)
 CHUNKS = len(SHARES)
 BLOCKS = 7
 PIECES = 3
@@ -88,7 +88,9 @@
     second_hbm,
     master_hbm,
     gath,
-    gradient_out,
+    moment_hbm_out,
+    second_hbm_out,
+    master_hbm_out,
     grads,
     moment,
     second,
@@ -109,6 +111,7 @@
     rep_dst,
     load_sem,
     adam_sem,
+    state_sem,
     up_ss,
     up_rs,
     dn_ss,
@@ -147,6 +150,12 @@
     ]
     for copy in adam_loads:
         copy.start()
+    state_stores = [
+        pltpu.make_async_copy(src, dst, state_sem.at[i])
+        for i, (src, dst) in enumerate(
+            ((moment, moment_hbm_out), (second, second_hbm_out), (master, master_hbm_out))
+        )
+    ]
 
     barrier = pltpu.get_barrier_semaphore()
 
@@ -317,8 +326,11 @@
                 master[:, cols],
                 kept,
             )
-            gradient_out[:, cols] = gradient[b * TILE : (b + 1) * TILE]
+            moment[:, cols], second[:, cols], master[:, cols] = new
             fresh.append(new[2].astype(BF16))
+        if k == CHUNKS - 1:
+            for copy in state_stores:
+                copy.start()
         tall = jnp.concatenate(fresh, axis=0)
         rep_src[k][...] = dot(collect_t[...], tall).astype(BF16).reshape(nodes, TILE, bws[k])
         send_nodes(k, rep_src, rep_dst, rep_ss, rep_rs)
@@ -518,6 +530,9 @@
             if 0 <= tick - depth < CHUNKS:
                 stages[depth](tick - depth)
 
+    for copy in state_stores:
+        copy.wait()
+
     for k in range(CHUNKS):
         wait_nodes(k, fwd_src, fwd_ss)
         wait_nodes(k, rep_src, rep_ss)
@@ -550,24 +565,19 @@
 
 def write_kernel(
     slot_ref,
-    touched_ref,
     rows_hbm,
-    gradient_hbm,
     moment_hbm,
     second_hbm,
     master_hbm,
     tok_hbm,
-    moment_out_hbm,
-    second_out_hbm,
-    master_out_hbm,
+    moment_out,
+    second_out,
+    master_out,
     rows,
-    states,
     tok,
-    news,
     rows_sem,
     state_sem,
     tok_sem,
-    new_sem,
 ):
     width = rows.shape[1]
     block = width // PIECES
@@ -576,39 +586,28 @@
         pltpu.make_async_copy(rows_hbm.at[:, c], rows.at[:, c], rows_sem.at[p])
         for p, c in enumerate(pieces)
     ]
-    state_loads = [
-        pltpu.make_async_copy(ref, states.at[i], state_sem.at[i])
-        for i, ref in enumerate((gradient_hbm, moment_hbm, second_hbm, master_hbm))
+    stores = [
+        pltpu.make_async_copy(src, dst, state_sem.at[i])
+        for i, (src, dst) in enumerate(
+            ((moment_hbm, moment_out), (second_hbm, second_out), (master_hbm, master_out))
+        )
     ]
-    for copy in row_loads + state_loads:
+    for copy in row_loads + stores:
         copy.start()
     shape = (rows.shape[0], tok.shape[0])
     chosen = jnp.where(iota(shape, 0) == slot_ref[...], 1.0, 0.0).astype(F32)
     select_t = chosen.T.astype(BF16)
-    kept = column(touched_ref[...].astype(F32), touched_ref.shape[1]) >= 0.0
-    stores = []
     for p, c in enumerate(pieces):
         row_loads[p].wait()
         tok[:, c] = dot(select_t, rows[:, c]).astype(BF16)
         stores.append(pltpu.make_async_copy(tok.at[:, c], tok_hbm.at[:, c], tok_sem.at[p]))
         stores[-1].start()
-    for copy in state_loads:
-        copy.wait()
-    for p, c in enumerate(pieces):
-        new = adam_rows(states[0, :, c], states[1, :, c], states[2, :, c], states[3, :, c], kept)
-        outs = (moment_out_hbm, second_out_hbm, master_out_hbm)
-        for i, (value, out) in enumerate(zip(new, outs)):
-            news[i, :, c] = value
-            stores.append(
-                pltpu.make_async_copy(news.at[i, :, c], out.at[:, c], new_sem.at[i, p])
-            )
-            stores[-1].start()
     for copy in stores:
         copy.wait()
 
 
-def write_out(token_slot, touched_ids, rows, gradient, moment, second, master):
-    tokens, touch = token_slot.shape[0], touched_ids.shape[0]
+def write_out(token_slot, rows, moment, second, master):
+    tokens, touch = token_slot.shape[0], moment.shape[0]
     list_len, width = rows.shape
     vmem = pl.BlockSpec(memory_space=pltpu.VMEM)
     hbm = pl.BlockSpec(memory_space=pltpu.HBM)
@@ -617,28 +616,17 @@
         write_kernel,
         out_shape=(jax.ShapeDtypeStruct((tokens, width), BF16),)
         + (jax.ShapeDtypeStruct((touch, width), F32),) * 3,
-        in_specs=[vmem] * 2 + [hbm] * 5,
+        in_specs=[vmem] + [hbm] * 4,
         out_specs=[hbm] * 4,
         scratch_shapes=[
             pltpu.VMEM((list_len, width), BF16),
-            pltpu.VMEM((4, touch, width), F32),
             pltpu.VMEM((tokens, width), BF16),
-            pltpu.VMEM((3, touch, width), F32),
             dma((PIECES,)),
-            dma((4,)),
+            dma((3,)),
             dma((PIECES,)),
-            dma((3, PIECES)),
         ],
         compiler_params=pltpu.CompilerParams(vmem_limit_bytes=56 * 1024 * 1024),
-    )(
-        token_slot.reshape(1, tokens),
-        touched_ids.reshape(1, touch),
-        rows,
-        gradient,
-        moment,
-        second,
-        master,
-    )
+    )(token_slot.reshape(1, tokens), rows, moment, second, master)
 
 
 def on_device(nodes, locals_, grads, token_slot, node_ids, touched_ids, owner_map, moment, second, master):
@@ -656,14 +644,14 @@
     line = tuple(pltpu.VMEM((last, slots, cw), BF16) for cw in cws)
     plane = tuple(pltpu.VMEM((nodes, TILE, cw // BLOCKS), BF16) for cw in cws)
     stacked = BLOCKS * slots
-    rows, gradient = pl.pallas_call(
+    rows, *states = pl.pallas_call(
         functools.partial(kernel, nodes, locals_, cap),
         out_shape=(
             jax.ShapeDtypeStruct((list_len, width), BF16),
-            jax.ShapeDtypeStruct((touch, width), F32),
-        ),
+        )
+        + (jax.ShapeDtypeStruct((touch, width), F32),) * 3,
         in_specs=[vmem] * 4 + [hbm] * 4,
-        out_specs=[vmem] * 2,
+        out_specs=[vmem] + [hbm] * 3,
         scratch_shapes=[
             pltpu.VMEM((tokens, width), BF16),
             pltpu.VMEM((touch, width), F32),
@@ -684,6 +672,7 @@
             plane,
             plane,
             dma((CHUNKS,)),
+            dma((3,)),
             dma((3,)),
             dma((CHUNKS, last)),
             dma((CHUNKS, last)),
@@ -710,7 +699,7 @@
         second,
         master,
     )
-    return write_out(token_slot, touched_ids, rows, gradient, moment, second, master)
+    return write_out(token_slot, rows, *states)
 
 
 def solution(mesh):

time: 44.1 us -> 73 us (1.66)
  Pallas kernels: 43.3 us -> 72.2 us
    pallas_call x1, Pallas kernels: 3.79 us -> 33.1 us  [write_out(): pl.pallas_call(write_kernel, out_shape=(jax.ShapeDtypeStruct((tokens, wid...]
where the time goes in v8:
time: 73 us; the launch traced here: 72.8 us
  Pallas kernels  72.2 us (99%)
    pallas_call x1, Pallas kernels, on_device(): pl.pallas_call(functools.partial(kernel, nodes, locals_, cap), out_shape=...  39.1 us
    pallas_call x1, Pallas kernels, write_out(): pl.pallas_call(write_kernel, out_shape=(jax.ShapeDtypeStruct((tokens, wid...  33.1 us

profile of v8, /device:TPU:0, one launch (start us, length us, event | category | flops | bytes accessed | tf_op | source)
XLA Modules:
  0.0 72.8 jit_solution(3601620508341850018)
XLA Ops:
  0.6 39.1 %shard_map.111 = (bf16[64,5376]{1,0:T(8,128)(2,1)}, f32[16,5376]{1,0:T(8,128)}, f32[16,5376]{1,0:T(8,128)}, f32[16,5376]{1,0:T(8,128)}) custom-call(s32[1,128]{1,0:T(1,128)} %bitcast.5, s32[1,16]{1,0:T(1,128)} %ids_ref.1, s32[1,16]{1,0:T(1,128)} %bitcast.8, s32[2,8]{1,0:T(2,128)} %bitcast.7, bf16[128,5376]{1,0:T(8,128)(2,1)} %grads_hbm.1, ...), custom_call_target="tpu_custom_call" | custom-call | tf_op jit(solution)/shard_map/pallas_call | solution.py:647
  39.7 33.1 %shard_map.112 = (bf16[128,5376]{1,0:T(8,128)(2,1)}, f32[16,5376]{1,0:T(8,128)}, f32[16,5376]{1,0:T(8,128)}, f32[16,5376]{1,0:T(8,128)}) custom-call(s32[1,128]{1,0:T(1,128)} %bitcast.6, bf16[64,5376]{1,0:T(8,128)(2,1)} %get-tuple-element.8.rows_hbm, f32[16,5376]{1,0:T(8,128)} %get-tuple-element.9.moment_hbm, f32[16,5376]{1,0:T(8,128)} %get-tuple-element.10.second_hbm, ...), custom_call_target="tpu_custom_call" | custom-call | tf_op jit(solution)/shard_map/pallas_call | solution.py:615
